TPU v7x, 32 devices: a whole 2x2x4 slice. The times are simulated.
32 devices in a mesh: groups: 2 (over x), tenant: 4 (over y, core), tensor: 4 (over z).
Axes of the slice: x: 2, y: 2, z: 4, core: 2. Of those that a mesh axis runs over, the one named last changes fastest.
Arguments:
- tokens: bfloat16 [6144, 8192], P(('groups', 'tenant')), parts along dimension 0, may hold values from -6 to 6
- kv_weight: bfloat16 [8192, 2, 1024], P(None, None, 'tensor'), may hold values from -0.0625 to 0.0625
- cotangent: bfloat16 [6144, 2, 1024], P(('groups', 'tenant'), None, 'tensor'), parts along dimension 0, may hold values from -4 to 4
- a_store: bfloat16 [24, 16, 8192], P('tenant', None, 'tensor'), may hold values from -0.0625 to 0.0625
- b_store: bfloat16 [24, 16, 2, 1024], P('tenant', None, None, 'tensor'), may hold values from -0.625 to 0.625
- tile_tenant: int32 [48], P(('groups', 'tenant')), parts along dimension 0, may hold values from 0 to 23
- tenant_place: int32 [24], replicated, may hold values from 0 to 23, each once
Outputs:
- kv_out: bfloat16 [6144, 2, 1024], P(('groups', 'tenant'), None, 'tensor'), parts along dimension 0
- input_grad: bfloat16 [6144, 8192], P(('groups', 'tenant'), 'tensor'), parts along dimension 0
- a_grad: float32 [48, 16, 8192], P(('groups', 'tenant'), None, 'tensor'), parts along dimension 0
- b_grad: float32 [48, 16, 2, 1024], P(('groups', 'tenant'), None, None, 'tensor'), parts along dimension 0
There are 2 independent parts, one for each index of `groups`. A program takes and returns all parts, laid end to end along the dimension named above; an argument that names none is the same for every part. Nothing has to cross between parts.
Inputs may be any that keep to these rules, and one draw needn't show every extreme that they name: `tile_tenant`: each tile of 128 rows belongs to one tenant. A permutation; the adapters of tenant t are stored at row tenant_place[t], on tenant index tenant_place[t] // 6.
All inputs are finite; a program needn't handle non-finite values.
Results may differ from a plain program's by a relative error of at most 0.014.
Values may be sent and summed in bfloat16 or wider, within the bound.
A program may use at most 128 MiB of HBM per device.

v0:
```python
import jax
import jax.numpy as jnp
from jax import lax
from jax.sharding import PartitionSpec as P


def local(tokens, kv_weight, cotangent, a_store, b_store, tile_tenant, tenant_place):
    adapter_scale = 2.0
    row_count, model_width = tokens.shape
    tile_count = tile_tenant.shape[0]
    tile_len = row_count // tile_count
    slot_count, rank_size, narrow = a_store.shape
    part_cols = kv_weight.shape[2]
    wide_cols = 2 * part_cols
    tenant_total = tenant_place.shape[0]
    column_start = lax.axis_index("tensor") * narrow
    x_cols = lax.dynamic_slice_in_dim(tokens, column_start, narrow, 1)
    lookup = tile_tenant[:, None] == jnp.arange(tenant_total, dtype=jnp.int32)[None, :]
    wanted = jnp.sum(jnp.where(lookup, tenant_place[None, :], 0), axis=1)
    pieces = (
        lax.all_gather(a_store, "tenant", axis=0, tiled=True),
        lax.all_gather(b_store, "tenant", axis=0, tiled=True),
    )
    piece_count = pieces[0].shape[0]
    select = (wanted[:, None] == jnp.arange(piece_count, dtype=jnp.int32)[None, :]).astype(
        jnp.bfloat16
    )
    a_part = jnp.einsum("jk,krd->jrd", select, pieces[0], preferred_element_type=jnp.float32)
    b_part = jnp.einsum(
        "jk,krc->jrc",
        select,
        pieces[1].reshape(piece_count, rank_size, wide_cols),
        preferred_element_type=jnp.float32,
    )
    a_sel = a_part.astype(jnp.bfloat16)
    b_sel = b_part.astype(jnp.bfloat16)
    input_tile_list = x_cols.reshape(tile_count, tile_len, narrow)
    g_flat = cotangent.reshape(row_count, wide_cols)
    gradient_tile_list = g_flat.reshape(tile_count, tile_len, wide_cols)
    shrink_part = jnp.einsum(
        "jtd,jrd->jtr", input_tile_list, a_sel, preferred_element_type=jnp.float32
    )
    back_part = jnp.einsum(
        "jtc,jrc->jtr", gradient_tile_list, b_sel, preferred_element_type=jnp.float32
    )
    shrink_sum, back_sum = (
        lax.psum(shrink_part.astype(jnp.bfloat16), "tensor").astype(jnp.float32),
        lax.psum(back_part.astype(jnp.bfloat16), "tensor").astype(jnp.float32),
    )
    rank_projection = shrink_sum.astype(jnp.bfloat16)
    backward_rank_product = back_sum.astype(jnp.bfloat16)
    w_flat = kv_weight.reshape(model_width, wide_cols)
    frozen_output = jnp.dot(tokens, w_flat, preferred_element_type=jnp.float32).reshape(
        tile_count, tile_len, wide_cols
    )
    adapter_output = frozen_output + adapter_scale * jnp.einsum(
        "zxg,zgk->zxk", rank_projection, b_sel, preferred_element_type=jnp.float32
    )
    kv_out = adapter_output.reshape(row_count, 2, part_cols).astype(jnp.bfloat16)
    partial_grad = lax.dot_general(
        g_flat, w_flat, (((1,), (1,)), ((), ())), preferred_element_type=jnp.float32
    )
    summed = lax.psum_scatter(
        partial_grad.astype(jnp.bfloat16), "tensor", scatter_dimension=1, tiled=True
    ).astype(jnp.float32)
    adapter_delta = adapter_scale * jnp.einsum(
        "xeg,xgl->xel", backward_rank_product, a_sel, preferred_element_type=jnp.float32
    )
    input_grad = (summed + adapter_delta.reshape(row_count, narrow)).astype(jnp.bfloat16)
    down_weight_gradient = adapter_scale * jnp.einsum(
        "kvz,kve->kze", backward_rank_product, input_tile_list, preferred_element_type=jnp.float32
    )
    up_weight_gradient = adapter_scale * jnp.einsum(
        "wzy,wzn->wyn", rank_projection, gradient_tile_list, preferred_element_type=jnp.float32
    )
    tile_grads = jnp.concatenate([down_weight_gradient, up_weight_gradient], axis=2)
    senders = lax.all_gather(wanted, "tenant", axis=0, tiled=True)
    party_count = lax.axis_size("tenant")
    owner_index = lax.axis_index("tenant")
    target = wanted // slot_count
    to_peer = (jnp.arange(party_count, dtype=jnp.int32)[:, None] == target[None, :]).astype(
        jnp.float32
    )
    outgoing = to_peer[:, :, None, None] * tile_grads[None]
    incoming = lax.all_to_all(
        outgoing.astype(jnp.bfloat16), "tenant", split_axis=0, concat_axis=0, tiled=True
    ).astype(outgoing.dtype)
    sender_slots = senders.reshape(party_count, tile_count)
    owned_rows = (
        sender_slots[:, :, None]
        == owner_index * slot_count + jnp.arange(slot_count, dtype=jnp.int32)[None, None, :]
    ).astype(jnp.float32)
    returned = jnp.einsum("pjs,pjrc->src", owned_rows, incoming, precision=lax.Precision.HIGHEST)
    a_grad = returned[:, :, :narrow]
    b_grad = returned[:, :, narrow:].reshape(slot_count, rank_size, 2, part_cols)
    return (kv_out, input_grad, a_grad, b_grad)


def solution(mesh):
    in_specs = (
        P(("groups", "tenant"), None),
        P(None, None, "tensor"),
        P(("groups", "tenant"), None, "tensor"),
        P("tenant", None, "tensor"),
        P("tenant", None, None, "tensor"),
        P(("groups", "tenant")),
        P(),
    )
    out_specs = (
        P(("groups", "tenant"), None, "tensor"),
        P(("groups", "tenant"), "tensor"),
        P(("groups", "tenant"), None, "tensor"),
        P(("groups", "tenant"), None, None, "tensor"),
    )
    return jax.shard_map(local, mesh=mesh, in_specs=in_specs, out_specs=out_specs, check_vma=False)
```

profile of v0, /device:TPU:0, one launch (start us, length us, event | category | flops | bytes accessed | tf_op | source)
XLA Modules:
  0.0 252.1 jit_solution(7207738157128085039)
XLA Ops:
  8.0 0.0 all-gather.2.cloned.1.call-start
  8.0 0.7 all-gather.2.cloned.1.call-update
  8.7 0.0 reduce-scatter.2.cloned.1.call-start
  8.8 13.1 %bitcast_convert_fusion = bf16[768,8192]{1,0:T(8,128)(2,1)} fusion(bf16[8192,2,256]{2,1,0:T(2,128)(2,1)} %param.8, bf16[768,2,256]{2,1,0:T(2,128)(2,1)} %param.9), kind=kOutput, calls=%fused_computation | convolution fusion | flops 6448742400 | bytes 21757952 | tf_op jit(solution)/shard_map/dot_general | solution.py:60
  21.9 0.0 reduce-scatter.2.cloned.1.call-update
  22.0 1.1 copy-done.3
  23.1 0.5 reshape_reshape.3
  23.6 0.0 copy-start
  23.6 0.0 copy-start.4
  23.6 0.0 copy-start.5
  23.6 0.0 copy-start.6
  23.6 14.6 %reshape.78 = bf16[8192,512,1]{1,0,2:T(8,128)(2,1)} reshape(bf16[8192,2,256]{2,1,0:T(2,128)(2,1)} %param.8) | data formatting | bytes 16777216 | tf_op jit(solution)/shard_map/reshape | solution.py:52
  38.2 8.0 %all_gather.10 = bf16[24,16,2,256]{3,1,2,0:T(8,128)(2,1)S(1)} all-gather(bf16[6,16,2,256]{3,1,2,0:T(8,128)(2,1)S(1)} %copy.57), channel_id=1, replica_groups=mesh['groups'=2,'tenant'=4,'tensor'=4] {'tenant'}, dimensions={0}, use_global_device_ids=true | all-gather | bytes 491520 | tf_op jit(solution)/shard_map/all_gather | solution.py:22
  46.2 0.3 copy.58
  46.5 0.3 reshape.70
  46.7 0.0 copy-done.5
  46.7 0.0 copy-done.6
  46.8 0.2 select_reduce_fusion
  47.0 0.2 fusion.12
  47.2 0.3 fusion.5
  47.5 2.1 constant_dynamic-slice_fusion
  49.7 0.0 all-gather.2.cloned.1.call-done
  49.7 3.5 %fusion.3 = bf16[6,16,2048]{2,0,1:T(8,128)(2,1)S(1)} fusion(bf16[24,16,2048]{2,1,0:T(8,128)(2,1)} %all-gather.2.cloned.1.call-done, s32[6]{0:T(128)S(1)} %select_reduce_fusion), kind=kOutput, calls=%fused_computation.9 | convolution fusion | flops 9437328 | bytes 1966104 | tf_op jit(solution)/shard_map/jk,krd->jrd/dot_general | solution.py:28
  53.2 0.8 copy-done.1
  54.0 0.9 convolution_convert_fusion
  54.9 22.1 %all-reduce.1 = (bf16[6,128,16]{1,2,0:T(8,128)(2,1)S(1)}, bf16[6,128,16]{1,2,0:T(8,128)(2,1)S(1)}) all-reduce(bf16[6,128,16]{1,2,0:T(8,128)(2,1)S(1)} %convolution_convert_fusion, bf16[6,128,16]{1,2,0:T(8,128)(2,1)S(1)} %fusion.5), channel_id=1, replica_groups=mesh['groups'=2,'tenant'=4,'tensor'=4] {'tensor'}, use_global_device_ids=true, to_apply=%region_1.2 | all-reduce | flops 24576 | bytes 98304 | tf_op jit(solution)/shard_map/psum | solution.py:47
  77.0 1.3 convolution_multiply_fusion.2
  78.4 0.5 convolution_multiply_fusion.1
  78.9 0.1 pad_maximum_fusion
  79.0 1.7 multiply_convert_fusion
  80.7 3.8 %all-to-all-start = ((bf16[4,6,16,2560]{3,2,1,0:T(8,128)(2,1)}), bf16[4,6,16,2560]{3,2,1,0:T(8,128)(2,1)S(1)}, u32[]{:S(2)}, u32[]{:S(2)}) async-start(bf16[4,6,16,2560]{3,2,1,0:T(8,128)(2,1)} %multiply_convert_fusion), calls=%async_computation.1 | async-start | bytes 3932160 | tf_op jit(solution)/shard_map/all_to_all | solution.py:85
  84.4 0.0 copy-start.7
  84.5 13.0 %fusion.18 = f32[6,128,512]{2,1,0:T(8,128)} fusion(bf16[6,128,8192]{2,1,0:T(8,128)(2,1)} %bitcast.38, bf16[8192,512,1]{1,0,2:T(8,128)(2,1)} %reshape.78), kind=kOutput, calls=%fused_computation.36 | convolution fusion | flops 6442450944 | bytes 22544384 | tf_op jit(solution)/shard_map/dot_general | solution.py:53
  97.4 0.6 dynamic-slice
  98.7 0.2 dynamic-update-slice
  98.9 9.7 %all-reduce = s32[24]{0:T(128)S(1)} all-reduce(s32[24]{0:T(128)S(1)} %dynamic-update-slice), channel_id=1, replica_groups=mesh['groups'=2,'tenant'=4,'tensor'=4] {'tenant'}, use_global_device_ids=true, to_apply=%add | all-reduce | flops 24 | bytes 192
  108.6 0.1 eq.64
  108.7 1.8 add_convert_fusion
  110.5 1.1 convert_element_type.51
  111.6 3.6 %convolution_multiply_fusion = f32[6,128,2048]{2,1,0:T(8,128)} fusion(bf16[6,128,16]{1,2,0:T(8,128)(2,1)S(1)} %get-tuple-element.25, bf16[6,16,2048]{2,0,1:T(8,128)(2,1)S(1)} %copy-done.2), kind=kOutput, calls=%fused_computation.5 | convolution fusion | flops 51904512 | bytes 6709248 | tf_op jit(solution)/shard_map/xeg,xgl->xel/dot_general | solution.py:66
  115.2 0.0 all-to-all-done
  115.2 3.7 %convolution_bitcast_fusion = f32[6,16,2560]{2,0,1:T(8,128)S(1)} fusion(bf16[4,6,16,2560]{3,2,1,0:T(8,128)(2,1)S(1)} %all-to-all-done, s32[4,6]{1,0:T(4,128)S(1)} %eq.64, s32[6]{0:T(128)S(1)} %iota_add_fusion), kind=kOutput, calls=%fused_computation.6 | convolution fusion | flops 11796624 | bytes 2949240 | tf_op jit(solution)/shard_map/pjs,pjrc->src/dot_general | solution.py:93
  118.9 0.1 slice.8
  119.0 1.3 copy.64
  120.3 0.1 reshape.84
  120.5 0.7 copy.66
  121.2 116.9 %reduce-scatter.2.cloned.1.call-done = bf16[768,2048]{1,0:T(8,128)(2,1)} async-done(((bf16[768,8192]{1,0:T(8,128)(2,1)}), bf16[768,2048]{1,0:T(8,128)(2,1)}) %reduce-scatter.2.cloned.1.call-update) | async-done | bytes 3145744 | tf_op jit(solution)/shard_map/reduce_scatter | solution.py:63
  238.1 6.6 %fusion.1 = bf16[768,2048]{1,0:T(8,128)(2,1)} fusion(f32[6,128,2048]{2,1,0:T(8,128)} %convolution_multiply_fusion, bf16[768,2048]{1,0:T(8,128)(2,1)} %reduce-scatter.2.cloned.1.call-done), kind=kLoop, calls=%fused_computation.3 | loop fusion | flops 4718592 | bytes 12582912 | tf_op jit(solution)/shard_map/convert_element_type | solution.py:69
  (13 shorter events, 0.1 us)
Async XLA Ops:
  8.0 41.7 %all-gather.2.cloned.1.call-start = ((), (), s32[]{:S(2)}) async-start(), calls=%async_computation.2 | async-start | bytes 1966080 | tf_op jit(solution)/shard_map/all_gather | solution.py:21
  8.7 229.4 %reduce-scatter.2.cloned.1.call-start = ((), (), s32[]{:S(2)}) async-start(), calls=%async_computation.3 | async-start | bytes 15728640 | tf_op jit(solution)/shard_map/reduce_scatter | solution.py:63
  21.9 1.1 copy-start.3
  23.6 23.7 %copy-start = (bf16[6,128,512]{2,1,0:T(8,128)(2,1)}, bf16[6,128,512]{2,1,0:T(8,128)(2,1)S(1)}, u32[]{:S(2)}) copy-start(bf16[6,128,512]{2,1,0:T(8,128)(2,1)S(1)} %reshape_reshape.3) | copy-start | bytes 2359300
  23.6 14.6 %copy-start.4 = (bf16[6,16,2,256]{3,2,1,0:T(2,128)(2,1)S(1)}, bf16[6,16,2,256]{3,2,1,0:T(2,128)(2,1)}, u32[]{:S(2)}) copy-start(bf16[6,16,2,256]{3,2,1,0:T(2,128)(2,1)} %param.11) | copy-start | bytes 294916
  23.6 23.2 %copy-start.5 = (s32[24]{0:T(128)S(1)}, s32[24]{0:T(128)}, u32[]{:S(2)}) copy-start(s32[24]{0:T(128)} %param.13) | copy-start | bytes 292
  23.6 23.2 %copy-start.6 = (s32[6]{0:T(128)S(1)}, s32[6]{0:T(128)}, u32[]{:S(2)}) copy-start(s32[6]{0:T(128)} %param.12) | copy-start | bytes 76
  53.2 0.8 copy-start.1
  80.7 34.6 %all-to-all-start = ((bf16[4,6,16,2560]{3,2,1,0:T(8,128)(2,1)}), bf16[4,6,16,2560]{3,2,1,0:T(8,128)(2,1)S(1)}, u32[]{:S(2)}, u32[]{:S(2)}) async-start(bf16[4,6,16,2560]{3,2,1,0:T(8,128)(2,1)} %multiply_convert_fusion), calls=%async_computation.1 | async-start | bytes 3932160 | tf_op jit(solution)/shard_map/all_to_all | solution.py:85
  84.4 13.0 %copy-start.7 = (u32[32]{0:T(128)S(1)}, u32[32]{0:T(128)}, u32[]{:S(2)}) copy-start(u32[32]{0:T(128)} %constant.33) | copy-start | bytes 388
  97.4 14.2 %copy-start.2 = (bf16[6,16,2048]{2,0,1:T(8,128)(2,1)S(1)}, bf16[6,16,2048]{2,0,1:T(8,128)(2,1)}, u32[]{:S(2)}) copy-start(bf16[6,16,2048]{2,0,1:T(8,128)(2,1)} %copy-done.1) | copy-start | bytes 1179652
Sparse Core Ops, SparseCore 0:
  10.4 22.3 all-gather.1
Sparse Core Ops, SparseCore 1:
  22.0 216.0 reduce-scatter.1
where the time goes:
time: 253 us; the launch traced here: 252 us
  waiting for transfers between devices  118 us (47%)
  matrix products  42 us (17%)
  blocking collectives  39.8 us (16%)
  local copies, waits for them, and re-layouts  24 us (9%)
  between operations  16.3 us (6%)
  other arithmetic  8.55 us (3%)
  starting transfers between devices  3.86 us (2%)
    reduce_scatter x1, waiting for transfers between devices, local(): lax.psum_scatter(partial_grad.astype(jnp.bfloat16), 'tensor', scatter_dim...  117 us
    psum x1, blocking collectives, local(): lax.psum(shrink_part.astype(jnp.bfloat16), 'tensor').astype(jnp.float32)  22.1 us
    reshape x1, local copies, waits for them, and re-layouts, local(): w_flat = kv_weight.reshape(model_width, wide_cols)  14.6 us
    dot_general x1, matrix products, local(): lax.dot_general(g_flat, w_flat, (((1,), (1,)), ((), ())), preferred_eleme...  13.1 us
    dot_general x1, matrix products, local(): jnp.dot(tokens, w_flat, preferred_element_type=jnp.float32)  13 us
    unnamed x1, blocking collectives  9.71 us
    all_gather x1, blocking collectives, local(): lax.all_gather(b_store, 'tenant', axis=0, tiled=True)  7.96 us
    convert_element_type x1, other arithmetic, local(): (summed + adapter_delta.reshape(row_count, narrow)).astype(jnp.bfloat16)  6.58 us
  transfers between devices with their start and end apart: 3, of which 1 were waited for; matrix products, arithmetic and copies ran while one was open for 26% of the time, Pallas kernels for 0%

commit v1 on v0

v1 whole, which is shorter than its diff:
```python
import jax
import jax.numpy as jnp
from jax import lax
from jax.sharding import PartitionSpec as P

F32 = jnp.float32
BF16 = jnp.bfloat16


def mm(a, b, ca, cb):
    return lax.dot_general(a, b, (((ca,), (cb,)), ((), ())), preferred_element_type=F32)


def local(tokens, kv_weight, cotangent, a_store, b_store, tile_tenant, tenant_place):
    rows, model_width = tokens.shape
    tiles = tile_tenant.shape[0]
    tile_len = rows // tiles
    slots, rank, narrow = a_store.shape
    part_cols = kv_weight.shape[2]
    wide = 2 * part_cols
    tenants = tenant_place.shape[0]
    n_tensor = lax.axis_size("tensor")
    n_tenant = lax.axis_size("tenant")
    n_plane = lax.axis_size("groups") * n_tenant
    my_tensor = lax.axis_index("tensor")
    my_plane = lax.axis_index("groups") * n_tenant + lax.axis_index("tenant")

    b_flat = b_store.reshape(slots, rank, wide)
    a_all = lax.all_gather(a_store, "tenant", axis=0, tiled=True).reshape(-1, narrow)
    b_all = lax.all_gather(b_flat, "tenant", axis=0, tiled=True).reshape(-1, wide)
    stored = a_all.shape[0] // rank

    w_flat = kv_weight.reshape(model_width, wide)
    piece = narrow // n_plane
    w_share = lax.dynamic_index_in_dim(
        w_flat.reshape(n_tensor, n_plane, piece, wide), my_plane, 1, keepdims=False
    )
    w_got = lax.all_to_all(w_share, "tensor", split_axis=0, concat_axis=0, tiled=True)
    w_rows = lax.all_gather(w_got, ("groups", "tenant"), axis=0, tiled=False)
    g_flat = cotangent.reshape(rows, wide)
    g_all = lax.all_gather(g_flat, "tensor", axis=0, tiled=False)

    lookup = tile_tenant[:, None] == jnp.arange(tenants, dtype=jnp.int32)[None, :]
    wanted = jnp.sum(jnp.where(lookup, tenant_place[None, :], 0), axis=1)
    wanted_rows = jnp.repeat(wanted, tile_len)
    mask = wanted_rows[:, None] == (jnp.arange(stored * rank, dtype=jnp.int32) // rank)[None, :]
    fold = (
        (jnp.arange(stored * rank, dtype=jnp.int32) % rank)[:, None]
        == jnp.arange(rank, dtype=jnp.int32)[None, :]
    ).astype(BF16)

    x_cols = lax.dynamic_slice_in_dim(tokens, my_tensor * narrow, narrow, 1)
    shrink_part = jnp.where(mask, mm(x_cols, a_all, 1, 1), 0.0).astype(BF16)
    back_part = jnp.where(mask, mm(g_flat, b_all, 1, 1), 0.0).astype(BF16)
    parts = jnp.concatenate(
        [mm(shrink_part, fold, 1, 0).astype(BF16), mm(back_part, fold, 1, 0).astype(BF16)], axis=1
    )
    sums = lax.psum(parts, "tensor")
    twice = sums + sums
    shrink2 = jnp.where(mask, mm(twice[:, :rank], fold, 1, 1), 0.0).astype(BF16)
    back2 = jnp.where(mask, mm(twice[:, rank:], fold, 1, 1), 0.0).astype(BF16)

    a_part = mm(back2, x_cols, 0, 0).reshape(n_tenant, slots * rank, narrow)
    b_part = mm(shrink2, g_flat, 0, 0).reshape(n_tenant, slots * rank, wide)
    grads = jnp.concatenate([a_part, b_part], axis=2).astype(BF16)
    arrived = lax.all_to_all(grads, "tenant", split_axis=0, concat_axis=0, tiled=True)
    summed = jnp.sum(arrived.astype(F32), axis=0)
    a_grad = summed[:, :narrow].reshape(slots, rank, narrow)
    b_grad = summed[:, narrow:].reshape(slots, rank, 2, part_cols)

    kv_out = (mm(tokens, w_flat, 1, 0) + mm(shrink2, b_all, 1, 0)).astype(BF16)
    kv_out = kv_out.reshape(rows, 2, part_cols)

    total = mm(back2, a_all, 1, 0)
    w_mine = w_rows.transpose(1, 0, 2, 3).reshape(n_tensor, narrow, wide)
    for block in range(n_tensor):
        total = total + mm(g_all[block], w_mine[block], 1, 1)
    input_grad = total.astype(BF16)
    return (kv_out, input_grad, a_grad, b_grad)


def solution(mesh):
    in_specs = (
        P(("groups", "tenant"), None),
        P(None, None, "tensor"),
        P(("groups", "tenant"), None, "tensor"),
        P("tenant", None, "tensor"),
        P("tenant", None, None, "tensor"),
        P(("groups", "tenant")),
        P(),
    )
    out_specs = (
        P(("groups", "tenant"), None, "tensor"),
        P(("groups", "tenant"), "tensor"),
        P(("groups", "tenant"), None, "tensor"),
        P(("groups", "tenant"), None, None, "tensor"),
    )
    return jax.shard_map(local, mesh=mesh, in_specs=in_specs, out_specs=out_specs, check_vma=False)
```

time: 253 us -> 203 us (0.80)
  waiting for transfers between devices: 118 us -> 49.9 us
  blocking collectives: 39.8 us -> 56.6 us
  local copies, waits for them, and re-layouts: 24 us -> 35.3 us
  other arithmetic: 8.55 us -> 1.9 us
    reduce_scatter x1 -> x0, waiting for transfers between devices: 117 us -> none  [local(): lax.psum_scatter(partial_grad.astype(jnp.bfloat16), 'tensor', scatter_dim...]
    all_gather x1 -> x3, waiting for transfers between devices: 0.02 us -> 39.2 us  [the longest x1 39.2 us: local(): g_all = lax.all_gather(g_flat, 'tensor', axis=0, tiled=False)]
    all_to_all x0 -> x1, blocking collectives: none -> 32.1 us  [local(): lax.all_to_all(w_share, 'tensor', split_axis=0, concat_axis=0, tiled=True)]
    another operation x1 -> x2, local copies, waits for them, and re-layouts: 0.5 us -> 15.5 us  [the longest x1 14.2 us: local(): w_flat.reshape(n_tensor, n_plane, piece, wide)]
    reshape x4 -> x3, local copies, waits for them, and re-layouts: 15.7 us -> 1.37 us  [the longest x1 0.8 us: local(): b_grad = summed[:, narrow:].reshape(slots, rank, 2, part_cols)]
    all_to_all x1, waiting for transfers between devices: 0.01 us -> 10 us  [local(): lax.all_to_all(grads, 'tenant', split_axis=0, concat_axis=0, tiled=True)]
    unnamed x1 -> x0, blocking collectives: 9.71 us -> none
    convert_element_type x3 -> x0, other arithmetic: 8.28 us -> none  [the longest x1 6.58 us: local(): (summed + adapter_delta.reshape(row_count, narrow)).astype(jnp.bfloat16)]
  transfers between devices with their start and end apart: 3 -> 4, of which waited for: 1 -> 2; matrix products, arithmetic and copies ran while one was open for 26% -> 29% of each run, Pallas kernels for 0% -> 0%
where the time goes in v1:
time: 203 us
  blocking collectives  56.6 us (28%)
  waiting for transfers between devices  49.9 us (25%)
  matrix products  41.1 us (20%)
  local copies, waits for them, and re-layouts  35.3 us (17%)
  between operations  14 us (7%)
  starting transfers between devices  3.9 us (2%)
    dot_general x13, matrix products, mm(): lax.dot_general(a, b, (((ca,), (cb,)), ((), ())), preferred_element_type=...  41.1 us
    all_gather x1, waiting for transfers between devices, local(): g_all = lax.all_gather(g_flat, 'tensor', axis=0, tiled=False)  39.2 us
    all_to_all x1, blocking collectives, local(): lax.all_to_all(w_share, 'tensor', split_axis=0, concat_axis=0, tiled=True)  32.1 us
    psum x1, blocking collectives, local(): sums = lax.psum(parts, 'tensor')  18 us
    another operation x1, local copies, waits for them, and re-layouts, local(): w_flat.reshape(n_tensor, n_plane, piece, wide)  14.2 us
    unnamed x19, local copies, waits for them, and re-layouts  10 us
    all_to_all x1, waiting for transfers between devices, local(): lax.all_to_all(grads, 'tenant', split_axis=0, concat_axis=0, tiled=True)  10 us
    all_gather x1, blocking collectives, local(): lax.all_gather(b_flat, 'tenant', axis=0, tiled=True).reshape(-1, wide)  6.53 us
  transfers between devices with their start and end apart: 4, of which 2 were waited for; matrix products, arithmetic and copies ran while one was open for 29% of the time, Pallas kernels for 0%

profile of v1, /device:TPU:0, one launch (start us, length us, event | category | flops | bytes accessed | tf_op | source)
XLA Modules:
  0.0 202.7 jit_solution(14592690228170228408)
XLA Ops:
  7.2 0.0 all-gather.5.cloned.1.call-start
  7.2 0.7 all-gather.5.cloned.1.call-update
  7.9 0.0 all-gather.9.cloned.1.call-start
  8.0 14.2 %reshape_reshape.3 = bf16[4,8,256,512]{3,2,1,0:T(8,128)(2,1)} reshape(bf16[8192,2,256]{2,1,0:T(2,128)(2,1)} %param.8) | data formatting | bytes 16777216 | tf_op jit(solution)/shard_map/reshape;reshape | solution.py:36
  22.1 1.3 dynamic-slice_bitcast_fusion
  23.4 0.0 copy-start.2
  23.4 32.1 %all_to_all.10 = bf16[4,256,512]{2,1,0:T(8,128)(2,1)} all-to-all(bf16[4,256,512]{2,1,0:T(8,128)(2,1)S(1)} %dynamic-slice_bitcast_fusion), channel_id=1, replica_groups=mesh['groups'=2,'tenant'=4,'tensor'=4] {'tensor'}, dimensions={0} | all-to-all | bytes 2097152 | tf_op jit(solution)/shard_map/all_to_all | solution.py:38
  55.5 0.0 all-gather.9.cloned.1.call-update
  55.5 0.0 copy-start.6
  55.5 0.0 copy-start.7
  55.5 0.0 copy-start.5
  55.5 0.0 all-gather.7.cloned.1.call-start
  55.6 1.4 all_gather_reshape.3
  57.0 0.0 all-gather.7.cloned.1.call-update
  57.0 0.5 reshape.82
  57.5 0.0 copy-done.6
  57.5 0.0 copy-done.7
  57.5 0.2 select_reduce_fusion
  57.7 0.1 broadcast_bitcast_fusion
  57.8 0.1 reshape.75
  57.9 6.5 %all_gather.16 = bf16[24,16,512]{2,1,0:T(8,128)(2,1)S(1)} all-gather(bf16[6,16,512]{2,1,0:T(8,128)(2,1)S(1)} %reshape.75), channel_id=1, replica_groups=mesh['groups'=2,'tenant'=4,'tensor'=4] {'tenant'}, dimensions={0}, use_global_device_ids=true | all-gather | bytes 491520 | tf_op jit(solution)/shard_map/all_gather | solution.py:30
  64.4 0.2 copy.37
  64.6 8.0 %copy.36 = bf16[1024,8,2,256]{3,1,2,0:T(8,128)(2,1)} copy(bf16[1024,8,2,256]{3,2,1,0:T(2,128)(2,1)} %bitcast.70) | data formatting | bytes 16777216
  72.6 0.7 fusion.20
  73.3 4.3 %fusion.17 = bf16[768,16]{0,1:T(8,128)(2,1)S(1)} fusion(bf16[384,2048]{1,0:T(8,128)(2,1)} %bitcast.81, bf16[768,8192]{1,0:T(8,128)(2,1)} %param.7, s32[]{:T(128)S(6)} %select_n.57, s32[384]{0:T(512)S(1)} %get-tuple-element.23, s32[768]{0:T(1024)S(1)} %broadcast_bitcast_fusion, s32[384]{0:T(512)S(1)} %get-tuple-element.22), kind=kOutput, calls=%fused_computation.25 | convolution fusion | flops 1218299904 | bytes 4749316 | tf_op jit(solution)/shard_map/dot_general | solution.py:11
  77.7 18.0 %psum.8 = bf16[768,32]{0,1:T(8,128)(2,1)S(1)} all-reduce(bf16[768,32]{0,1:T(8,128)(2,1)S(1)} %maximum_add_fusion), channel_id=1, replica_groups=mesh['groups'=2,'tenant'=4,'tensor'=4] {'tensor'}, use_global_device_ids=true, to_apply=%region_1.2 | all-reduce | flops 24576 | bytes 98304 | tf_op jit(solution)/shard_map/psum | solution.py:58
  95.7 0.4 fusion.10
  96.1 0.4 fusion.16
  96.5 0.5 convolution_convert_fusion.1
  97.0 3.3 %convolution_convert_fusion = bf16[384,2048]{1,0:T(8,128)(2,1)S(1)} fusion(bf16[768,384]{1,0:T(8,128)(2,1)S(1)} %fusion.10, bf16[768,8192]{1,0:T(8,128)(2,1)} %param.7, s32[]{:T(128)S(6)} %select_n.57), kind=kOutput, calls=%fused_computation.6 | convolution fusion | flops 1208745984 | bytes 5308420 | tf_op jit(solution)/shard_map/dot_general | solution.py:11
  100.3 1.4 pad_maximum_fusion
  101.7 3.8 %all-to-all-start.1 = ((bf16[4,96,2560]{2,1,0:T(8,128)(2,1)}), bf16[4,96,2560]{2,1,0:T(8,128)(2,1)S(1)}, u32[]{:S(2)}, u32[]{:S(2)}) async-start(bf16[4,96,2560]{2,1,0:T(8,128)(2,1)} %pad_maximum_fusion), calls=%async_computation.1 | async-start | bytes 3932160 | tf_op jit(solution)/shard_map/all_to_all | solution.py:66
  105.5 0.3 copy.24
  105.8 0.7 fusion.25
  106.5 11.2 %add_convert_fusion = bf16[768,512]{0,1:T(8,128)(2,1)S(1)} fusion(f32[768,512]{0,1:T(8,128)S(1)} %fusion.25, bf16[768,8192]{1,0:T(8,128)(2,1)} %param.7, bf16[8192,512]{1,0:T(8,128)(2,1)} %bitcast.76), kind=kOutput, calls=%fused_computation.15 | convolution fusion | flops 6443237376 | bytes 23330816 | tf_op jit(solution)/shard_map/dot_general | solution.py:11
  117.8 1.8 copy.30
  119.6 10.0 %all-to-all-done.1 = bf16[4,96,2560]{2,1,0:T(8,128)(2,1)S(1)} async-done(((bf16[4,96,2560]{2,1,0:T(8,128)(2,1)}), bf16[4,96,2560]{2,1,0:T(8,128)(2,1)S(1)}, u32[]{:S(2)}, u32[]{:S(2)}) %all-to-all-start.1) | async-done | bytes 1966112 | tf_op jit(solution)/shard_map/all_to_all | solution.py:66
  129.6 0.3 convert_reduce_fusion
  129.8 0.9 slice.62
  130.8 0.8 reshape.80
  131.6 5.7 %fusion.56 = (bf16[1,8,256,512]{3,2,0,1:T(8,128)(2,1)}, bf16[1,8,256,512]{3,2,0,1:T(8,128)(2,1)}, bf16[1,8,256,512]{3,2,0,1:T(8,128)(2,1)S(1)}, bf16[1,8,256,512]{3,2,0,1:T(8,128)(2,1)}) fusion(bf16[4,8,256,512]{3,2,0,1:T(8,128)(2,1)} %bitcast.75), kind=kLoop, calls=%fused_computation.74 | loop fusion | bytes 16777216 | tf_op jit(solution)/shard_map/slice | solution.py:77
  137.3 39.2 %all-gather.7.cloned.1.call-done = bf16[4,768,512]{2,1,0:T(8,128)(2,1)} async-done(((bf16[1,768,512]{2,1,0:T(8,128)(2,1)}), bf16[4,768,512]{2,1,0:T(8,128)(2,1)}) %all-gather.7.cloned.1.call-update) | async-done | bytes 3145744 | tf_op jit(solution)/shard_map/all_gather | solution.py:41
  176.5 3.7 %fusion.21 = f32[2048,768]{0,1:T(8,128)S(1)} fusion(bf16[2048,512]{1,0:T(8,128)(2,1)} %bitcast.74, bf16[4,768,512]{2,1,0:T(8,128)(2,1)} %all-gather.7.cloned.1.call-done), kind=kOutput, calls=%fused_computation.29 | convolution fusion | flops 1610612736 | bytes 9175040 | tf_op jit(solution)/shard_map/dot_general | solution.py:11
  180.3 1.8 fusion.22
  182.1 0.0 copy-start
  182.2 1.8 fusion.23
  184.0 4.5 %fusion.24 = f32[2048,768]{0,1:T(8,128)} fusion(bf16[2048,512]{1,0:T(8,128)(2,1)S(1)} %bitcast.71, bf16[4,768,512]{2,1,0:T(8,128)(2,1)S(1)} %copy-done.3), kind=kOutput, calls=%fused_computation.35 | convolution fusion | flops 1610612736 | bytes 9175040 | tf_op jit(solution)/shard_map/dot_general | solution.py:11
  188.5 7.7 %fusion = bf16[768,2048]{1,0:T(8,128)(2,1)} fusion(f32[2048,768]{0,1:T(8,128)S(1)} %fusion.21, f32[2048,768]{0,1:T(8,128)S(1)} %fusion.22, f32[2048,768]{0,1:T(8,128)S(1)} %fusion.23, f32[2048,768]{0,1:T(8,128)} %fusion.24, bf16[768,384]{1,0:T(8,128)(2,1)} %copy-done.4, bf16[384,2048]{1,0:T(8,128)(2,1)} %bitcast.82), kind=kOutput, calls=%fused_computation.1 | convolution fusion | flops 1215823872 | bytes 30474240 | tf_op jit(solution)/shard_map/dot_general | solution.py:11
  (14 shorter events, 0.1 us)
Async XLA Ops:
  7.2 66.2 %all-gather.5.cloned.1.call-start = ((), (), s32[]{:S(2)}) async-start(), calls=%async_computation.2 | async-start | bytes 1966080 | tf_op jit(solution)/shard_map/all_gather | solution.py:29
  7.9 123.7 %all-gather.9.cloned.1.call-start = ((), (), s32[]{:S(2)}) async-start(), calls=%async_computation.4 | async-start | bytes 9437184 | tf_op jit(solution)/shard_map/all_gather | solution.py:39
  23.4 32.2 %copy-start.2 = (bf16[768,2,256]{2,1,0:T(2,128)(2,1)S(1)}, bf16[768,2,256]{2,1,0:T(2,128)(2,1)}, u32[]{:S(2)}) copy-start(bf16[768,2,256]{2,1,0:T(2,128)(2,1)} %param.9) | copy-start | bytes 2359300
  55.5 2.0 %copy-start.6 = (s32[24]{0:T(128)S(1)}, s32[24]{0:T(128)}, u32[]{:S(2)}) copy-start(s32[24]{0:T(128)} %param.13) | copy-start | bytes 292
  55.5 2.0 %copy-start.7 = (s32[6]{0:T(128)S(1)}, s32[6]{0:T(128)}, u32[]{:S(2)}) copy-start(s32[6]{0:T(128)} %param.12) | copy-start | bytes 76
  55.5 2.3 %copy-start.5 = (bf16[6,16,2,256]{3,2,1,0:T(2,128)(2,1)S(1)}, bf16[6,16,2,256]{3,2,1,0:T(2,128)(2,1)}, u32[]{:S(2)}) copy-start(bf16[6,16,2,256]{3,2,1,0:T(2,128)(2,1)} %param.11) | copy-start | bytes 294916
  55.5 121.0 %all-gather.7.cloned.1.call-start = ((), (), s32[]{:S(2)}) async-start(), calls=%async_computation.3 | async-start | bytes 3932160 | tf_op jit(solution)/shard_map/all_gather | solution.py:41
  96.1 4.2 %copy-start.4 = (bf16[768,384]{1,0:T(8,128)(2,1)}, bf16[768,384]{1,0:T(8,128)(2,1)S(1)}, u32[]{:S(2)}) copy-start(bf16[768,384]{1,0:T(8,128)(2,1)S(1)} %fusion.10) | copy-start | bytes 1769476
  101.7 27.9 %all-to-all-start.1 = ((bf16[4,96,2560]{2,1,0:T(8,128)(2,1)}), bf16[4,96,2560]{2,1,0:T(8,128)(2,1)S(1)}, u32[]{:S(2)}, u32[]{:S(2)}) async-start(bf16[4,96,2560]{2,1,0:T(8,128)(2,1)} %pad_maximum_fusion), calls=%async_computation.1 | async-start | bytes 3932160 | tf_op jit(solution)/shard_map/all_to_all | solution.py:66
  176.5 3.7 %copy-start.3 = (bf16[4,768,512]{2,1,0:T(8,128)(2,1)S(1)}, bf16[4,768,512]{2,1,0:T(8,128)(2,1)}, u32[]{:S(2)}) copy-start(bf16[4,768,512]{2,1,0:T(8,128)(2,1)} %all-gather.7.cloned.1.call-done) | copy-start | bytes 9437188
  180.3 1.8 copy-start.1
  182.1 1.8 copy-start
Sparse Core Ops, SparseCore 0:
  9.6 22.3 all-gather.4
  55.6 53.5 all-gather.8
  110.8 65.7 all-gather.6

commit v2 on v1

v2 whole, which is shorter than its diff:
```python
import functools
import jax
import jax.numpy as jnp
from jax import lax
from jax.experimental import pallas as pl
from jax.experimental.pallas import tpu as pltpu
from jax.sharding import PartitionSpec as P

F32 = jnp.float32
BF16 = jnp.bfloat16
MESH = pl.DeviceIdType.MESH


def mm(a, b, ca, cb):
    return lax.dot_general(a, b, (((ca,), (cb,)), ((), ())), preferred_element_type=F32)


def kernel(
    sizes, tokens, weight, g_ref, a_ref, b_ref, want_ref,
    kv_ref, in_ref, ag_ref, bg_ref,
    x_buf, wk_buf, acc, x_cols, w_buf, g_buf, total, rank_out, rank_in, grad_out, grad_in, back_ref,
    x_sem, wk_sem, own_sem, w_send, w_recv, plane_send, sib_send,
    up_send, up_recv, down_send, down_recv, rank_send, rank_recv, grad_send, grad_recv,
):
    n, ng, nt, piece, rank, step = sizes
    rows, width = tokens.shape
    wide = weight.shape[1]
    narrow = x_cols.shape[1]
    stored = a_ref.shape[0]
    owned = stored // nt
    me = lax.axis_index("tensor")
    grp = lax.axis_index("groups")
    ten = lax.axis_index("tenant")
    plane = grp * nt + ten
    side = ten + 1 - 2 * lax.rem(ten, 2)

    def at_tensor(z):
        return (grp, ten, z)

    def line(k):
        return lax.rem(me + k, n)

    def mate(dg, dt):
        return lax.rem(grp + dg, ng), lax.rem(ten + dt, nt)

    barrier = pltpu.get_barrier_semaphore()
    for k in range(1, n):
        pl.semaphore_signal(barrier, inc=1, device_id=at_tensor(line(k)), device_id_type=MESH)
    for dg in range(ng):
        for dt in range(nt):
            if dg or dt:
                g2, t2 = mate(dg, dt)
                pl.semaphore_signal(barrier, inc=1, device_id=(g2, t2, me), device_id_type=MESH)

    def load(c, slot):
        return (
            pltpu.make_async_copy(
                tokens.at[:, pl.ds(pl.multiple_of(c * step, step), step)], x_buf.at[slot], x_sem.at[slot]
            ),
            pltpu.make_async_copy(
                weight.at[pl.ds(pl.multiple_of(c * step, step), step), :], wk_buf.at[slot], wk_sem.at[slot]
            ),
        )

    base = pl.multiple_of(me * narrow, narrow)
    own_x = pltpu.make_async_copy(tokens.at[:, pl.ds(base, narrow)], x_cols, own_sem.at[0])
    own_w = pltpu.make_async_copy(weight.at[pl.ds(base, narrow), :], w_buf.at[me], own_sem.at[1])
    own_x.start()
    for copy in load(0, 0):
        copy.start()
    own_w.start()
    pl.semaphore_wait(barrier, n - 1 + ng * nt - 1)

    def spot(z, p):
        return w_buf.at[z, pl.ds(pl.multiple_of(p * piece, piece), piece), :]

    def remote(src, dst, send, recv, device):
        return pltpu.make_async_remote_copy(
            src_ref=src, dst_ref=dst, send_sem=send, recv_sem=recv, device_id=device, device_id_type=MESH
        )

    w_sends = []
    for k in range(1, n):
        z = line(k)
        start = pl.multiple_of(z * narrow + plane * piece, piece)
        copy = remote(
            weight.at[pl.ds(start, piece), :], spot(me, plane), w_send.at[k], w_recv.at[me, plane], at_tensor(z)
        )
        copy.start()
        w_sends.append(copy)

    def up(s):
        o = jnp.maximum(me - s, 0)
        src = g_ref if s == 0 else g_buf.at[o]
        return (
            jnp.logical_and(me >= s, me < n - 1),
            remote(src, g_buf.at[o], up_send.at[s], up_recv.at[s], at_tensor(jnp.minimum(me + 1, n - 1))),
        )

    def down(s):
        o = jnp.minimum(me + s, n - 1)
        src = g_ref if s == 0 else g_buf.at[o]
        return (
            jnp.logical_and(me + s < n, me > 0),
            remote(src, g_buf.at[o], down_send.at[s], down_recv.at[s], at_tensor(jnp.maximum(me - 1, 0))),
        )

    def push(s):
        for ok, copy in (up(s), down(s)):
            pl.when(ok)(copy.start)

    def arrived(s):
        low, high = me - 1 - s, me + 1 + s
        pl.when(low >= 0)(
            remote(g_ref, g_buf.at[jnp.maximum(low, 0)], up_send.at[s], up_recv.at[s], at_tensor(jnp.maximum(me - 1, 0))).wait_recv
        )
        pl.when(high < n)(
            remote(g_ref, g_buf.at[jnp.minimum(high, n - 1)], down_send.at[s], down_recv.at[s], at_tensor(jnp.minimum(me + 1, n - 1))).wait_recv
        )

    push(0)

    ids = lax.broadcasted_iota(jnp.int32, (stored, rows), 0) // rank
    mask = ids == want_ref[...]
    fold = (
        lax.rem(lax.broadcasted_iota(jnp.int32, (stored, rank), 0), rank)
        == lax.broadcasted_iota(jnp.int32, (stored, rank), 1)
    ).astype(BF16)
    own_x.wait()
    part = jnp.where(mask, mm(a_ref[...], x_cols[...], 1, 1), 0.0).astype(BF16)
    rank_out[:rank, :] = mm(fold, part, 0, 0).astype(BF16)
    part = jnp.where(mask, mm(b_ref[...], g_ref[...], 1, 1), 0.0).astype(BF16)
    rank_out[rank:, :] = mm(fold, part, 0, 0).astype(BF16)
    rank_sends = []
    for k in range(1, n):
        copy = remote(rank_out, rank_in.at[me], rank_send.at[k], rank_recv.at[me], at_tensor(line(k)))
        copy.start()
        rank_sends.append(copy)

    chunks = width // step
    acc[...] = jnp.zeros_like(acc)

    def chunk(c, carry):
        slot = lax.rem(c, 2)

        @pl.when(c + 1 < chunks)
        def _():
            for copy in load(c + 1, 1 - slot):
                copy.start()

        for copy in load(c, slot):
            copy.wait()
        acc[...] += mm(x_buf[slot], wk_buf[slot], 1, 0)
        return carry

    lax.fori_loop(0, chunks, chunk, 0)

    plane_sends, sib_sends = [], []

    def to_side(z, p, i):
        copy = remote(spot(z, p), spot(z, p), sib_send.at[i], w_recv.at[z, p], (grp, side, me))
        copy.start()
        sib_sends.append(copy)

    def wait_piece(z, p):
        remote(spot(z, p), spot(z, p), sib_send.at[0], w_recv.at[z, p], (grp, side, me)).wait_recv()

    others = [(dg, dt) for dg in range(ng) for dt in range(0, nt, 2) if dg or dt]
    for k in range(1, n):
        z = line(k)
        wait_piece(z, plane)
        for dg, dt in others:
            g2, t2 = mate(dg, dt)
            copy = remote(
                spot(z, plane), spot(z, plane), plane_send.at[len(plane_sends)], w_recv.at[z, plane], (g2, t2, me)
            )
            copy.start()
            plane_sends.append(copy)
        to_side(z, plane, len(sib_sends))

    rank_in[me] = rank_out[...]
    for k in range(1, n):
        z = line(k)
        remote(rank_out, rank_in.at[z], rank_send.at[k], rank_recv.at[z], at_tensor(z)).wait_recv()
    whole = rank_in[0].astype(F32)
    for z in range(1, n):
        whole = whole + rank_in[z].astype(F32)
    twice = (whole.astype(BF16).astype(F32) * 2.0).astype(BF16)
    shrink = jnp.where(mask, mm(fold, twice[:rank, :], 1, 0), 0.0).astype(BF16)
    back_ref[...] = jnp.where(mask, mm(fold, twice[rank:, :], 1, 0), 0.0).astype(BF16)

    for p in range(nt):
        part_rows = pl.ds(p * owned, owned)
        grad_out[p, :, :narrow] = mm(back_ref[part_rows, :], x_cols[...], 1, 0).astype(BF16)
    spread = mm(shrink, g_ref[...], 1, 0).astype(BF16)
    for p in range(nt):
        grad_out[p, :, narrow:] = spread[p * owned : (p + 1) * owned, :]
    grad_sends = []
    for dt in range(1, nt):
        t2 = lax.rem(ten + dt, nt)
        copy = remote(grad_out.at[t2], grad_in.at[ten], grad_send.at[dt], grad_recv.at[ten], (grp, t2, me))
        copy.start()
        grad_sends.append(copy)
    kv_ref[...] = (acc[...] + mm(shrink, b_ref[...], 0, 0)).astype(BF16)

    tile = min(narrow, 512)

    def add_block(o, g_block, first):
        def body(c, carry):
            cols = pl.ds(pl.multiple_of(c * tile, tile), tile)
            term = mm(g_block[...], w_buf[o, cols, :], 1, 1)
            if first:
                total[:, cols] = term + mm(back_ref[...], a_ref[:, cols], 0, 0)
            else:
                total[:, cols] += term
            return carry

        lax.fori_loop(0, narrow // tile, body, 0)

    own_w.wait()
    arrived(0)
    if n > 2:
        push(1)
    add_block(me, g_ref, True)
    for k in range(1, n):
        z = line(k)
        for dg, dt in others:
            g2, t2 = mate(dg, dt)
            p = g2 * nt + t2
            wait_piece(z, p)
            to_side(z, p, len(sib_sends))
    for s in range(1, n - 2):
        arrived(s)
        push(s + 1)
    for k in range(1, n):
        z = line(k)
        for dg in range(ng):
            for dt in range(0, nt, 2):
                g2 = lax.rem(grp + dg, ng)
                t2 = lax.rem(side + dt, nt)
                wait_piece(z, g2 * nt + t2)

    def use(s):
        low, high = me - 1 - s, me + 1 + s

        @pl.when(low >= 0)
        def _():
            o = jnp.maximum(low, 0)
            add_block(o, g_buf.at[o], False)

        @pl.when(high < n)
        def _():
            o = jnp.minimum(high, n - 1)
            add_block(o, g_buf.at[o], False)

    for s in range(n - 2):
        use(s)

    grad_in[ten] = grad_out[ten]
    for dt in range(1, nt):
        t2 = lax.rem(ten + dt, nt)
        remote(grad_out.at[t2], grad_in.at[t2], grad_send.at[dt], grad_recv.at[t2], (grp, t2, me)).wait_recv()
    ag = grad_in[0, :, :narrow].astype(F32)
    bg = grad_in[0, :, narrow:].astype(F32)
    for p in range(1, nt):
        ag = ag + grad_in[p, :, :narrow].astype(F32)
        bg = bg + grad_in[p, :, narrow:].astype(F32)
    ag_ref[...] = ag
    bg_ref[...] = bg

    arrived(n - 2)
    use(n - 2)
    in_ref[...] = total[...].astype(BF16)

    for copy in w_sends + plane_sends + sib_sends + rank_sends + grad_sends:
        copy.wait_send()
    for s in range(n - 1):
        for ok, copy in (up(s), down(s)):
            pl.when(ok)(copy.wait_send)


def local(tokens, kv_weight, cotangent, a_store, b_store, tile_tenant, tenant_place):
    rows, model_width = tokens.shape
    tiles = tile_tenant.shape[0]
    tile_len = rows // tiles
    slots, rank, narrow = a_store.shape
    part_cols = kv_weight.shape[2]
    wide = 2 * part_cols
    tenants = tenant_place.shape[0]
    n = lax.axis_size("tensor")
    nt = lax.axis_size("tenant")
    ng = lax.axis_size("groups")
    piece = narrow // (ng * nt)

    a_all = lax.all_gather(a_store, "tenant", axis=0, tiled=True).reshape(-1, narrow)
    b_all = lax.all_gather(b_store.reshape(slots, rank, wide), "tenant", axis=0, tiled=True).reshape(-1, wide)
    stored = a_all.shape[0]
    w_flat = kv_weight.reshape(model_width, wide)
    g_flat = cotangent.reshape(rows, wide)
    lookup = tile_tenant[:, None] == jnp.arange(tenants, dtype=jnp.int32)[None, :]
    wanted = jnp.sum(jnp.where(lookup, tenant_place[None, :], 0), axis=1)
    want_rows = jnp.repeat(wanted, tile_len)[None, :]

    step = 1024 if model_width % 1024 == 0 else model_width // 2
    vmem = pl.BlockSpec(memory_space=pltpu.VMEM)
    hbm = pl.BlockSpec(memory_space=pl.ANY)
    dma = pltpu.SemaphoreType.DMA
    mates = ng * nt // 2
    kv, inp, ag, bg = pl.pallas_call(
        functools.partial(kernel, (n, ng, nt, piece, rank, step)),
        out_shape=(
            jax.ShapeDtypeStruct((rows, wide), BF16),
            jax.ShapeDtypeStruct((rows, narrow), BF16),
            jax.ShapeDtypeStruct((slots * rank, narrow), F32),
            jax.ShapeDtypeStruct((slots * rank, wide), F32),
        ),
        in_specs=[hbm, hbm, vmem, vmem, vmem, vmem],
        out_specs=(vmem, vmem, vmem, vmem),
        scratch_shapes=[
            pltpu.VMEM((2, rows, step), BF16),
            pltpu.VMEM((2, step, wide), BF16),
            pltpu.VMEM((rows, wide), F32),
            pltpu.VMEM((rows, narrow), BF16),
            pltpu.VMEM((n, narrow, wide), BF16),
            pltpu.VMEM((n, rows, wide), BF16),
            pltpu.VMEM((rows, narrow), F32),
            pltpu.VMEM((2 * rank, rows), BF16),
            pltpu.VMEM((n, 2 * rank, rows), BF16),
            pltpu.VMEM((nt, slots * rank, narrow + wide), BF16),
            pltpu.VMEM((nt, slots * rank, narrow + wide), BF16),
            pltpu.VMEM((stored, rows), BF16),
            dma((2,)),
            dma((2,)),
            dma((2,)),
            dma((n,)),
            dma((n, ng * nt)),
            dma(((n - 1) * max(mates - 1, 1),)),
            dma(((n - 1) * mates,)),
            dma((n,)),
            dma((n,)),
            dma((n,)),
            dma((n,)),
            dma((n,)),
            dma((n,)),
            dma((nt,)),
            dma((nt,)),
        ],
        compiler_params=pltpu.CompilerParams(
            collective_id=0, has_side_effects=True, vmem_limit_bytes=60 * 1024 * 1024
        ),
    )(tokens, w_flat, g_flat, a_all, b_all, want_rows)
    return (
        kv.reshape(rows, 2, part_cols),
        inp,
        ag.reshape(slots, rank, narrow),
        bg.reshape(slots, rank, 2, part_cols),
    )


def solution(mesh):
    in_specs = (
        P(("groups", "tenant"), None),
        P(None, None, "tensor"),
        P(("groups", "tenant"), None, "tensor"),
        P("tenant", None, "tensor"),
        P("tenant", None, None, "tensor"),
        P(("groups", "tenant")),
        P(),
    )
    out_specs = (
        P(("groups", "tenant"), None, "tensor"),
        P(("groups", "tenant"), "tensor"),
        P(("groups", "tenant"), None, "tensor"),
        P(("groups", "tenant"), None, None, "tensor"),
    )
    return jax.shard_map(local, mesh=mesh, in_specs=in_specs, out_specs=out_specs, check_vma=False)
```

time: 203 us -> 145 us (0.71)
  Pallas kernels: 0 us -> 94.3 us
  waiting for transfers between devices: 49.9 us -> 3.59 us
  blocking collectives: 56.6 us -> 10.5 us
  matrix products: 41.1 us -> 0 us
  local copies, waits for them, and re-layouts: 35.3 us -> 21.4 us
  starting transfers between devices: 3.9 us -> 0.04 us
    pallas_call x0 -> x1, Pallas kernels: none -> 94.3 us  [local(): pl.pallas_call(functools.partial(kernel, (n, ng, nt, piece, rank, step)),...]
    dot_general x13 -> x0, matrix products: 41.1 us -> none  [mm(): lax.dot_general(a, b, (((ca,), (cb,)), ((), ())), preferred_element_type=...]
    all_gather x2 -> x0, waiting for transfers between devices: 39.2 us -> none  [the longest x1 39.2 us: local(): g_all = lax.all_gather(g_flat, 'tensor', axis=0, tiled=False)]
    all_to_all x1 -> x0, blocking collectives: 32.1 us -> none  [local(): lax.all_to_all(w_share, 'tensor', split_axis=0, concat_axis=0, tiled=True)]
    psum x1 -> x0, blocking collectives: 18 us -> none  [local(): sums = lax.psum(parts, 'tensor')]
    another operation x2 -> x0, local copies, waits for them, and re-layouts: 15.5 us -> none  [the longest x1 14.2 us: local(): w_flat.reshape(n_tensor, n_plane, piece, wide)]
    all_to_all x1 -> x0, waiting for transfers between devices: 10 us -> none  [local(): lax.all_to_all(grads, 'tenant', split_axis=0, concat_axis=0, tiled=True)]
    slice x3 -> x0, local copies, waits for them, and re-layouts: 6.66 us -> none  [the longest x1 5.71 us: local(): total = total + mm(g_all[block], w_mine[block], 1, 1)]
  transfers between devices with their start and end apart: 4 -> 1, of which waited for: 2 -> 1; matrix products, arithmetic and copies ran while one was open for 29% -> 9% of each run, Pallas kernels for 0% -> 0%
where the time goes in v2:
time: 145 us
  Pallas kernels  94.3 us (65%)
  local copies, waits for them, and re-layouts  21.4 us (15%)
  between operations  14 us (10%)
  blocking collectives  10.5 us (7%)
  waiting for transfers between devices  3.59 us (2%)
    pallas_call x1, Pallas kernels, local(): pl.pallas_call(functools.partial(kernel, (n, ng, nt, piece, rank, step)),...  94.3 us
    unnamed x8, local copies, waits for them, and re-layouts  15.8 us
    all_gather x1, blocking collectives, local(): lax.all_gather(b_store.reshape(slots, rank, wide), 'tenant', axis=0, tile...  10.5 us
    reshape x1, local copies, waits for them, and re-layouts, local(): kv.reshape(rows, 2, part_cols)  2.99 us
    all_gather x1, waiting for transfers between devices, local(): lax.all_gather(a_store, 'tenant', axis=0, tiled=True).reshape(-1, narrow)  2.91 us
  transfers between devices with their start and end apart: 1, of which 1 were waited for; matrix products, arithmetic and copies ran while one was open for 9% of the time, Pallas kernels for 0%

profile of v2, /device:TPU:0, one launch (start us, length us, event | category | flops | bytes accessed | tf_op | source)
XLA Modules:
  0.0 144.8 jit_solution(16791370634681070735)
XLA Ops:
  7.2 0.0 all-gather.2.cloned.1.call-start
  7.2 0.7 all-gather.2.cloned.1.call-update
  7.9 0.9 select_reduce_fusion
  8.8 0.1 broadcast_bitcast_fusion
  8.8 0.6 copy.15
  9.4 1.0 reshape.37
  10.4 2.2 %copy.12 = bf16[96,8,2,256]{3,1,2,0:T(8,128)(2,1)} copy(bf16[96,8,2,256]{3,2,1,0:T(2,128)(2,1)} %bitcast.18) | data formatting | bytes 1572864
  12.6 8.1 %copy.11 = bf16[1024,8,2,256]{3,1,2,0:T(8,128)(2,1)} copy(bf16[1024,8,2,256]{3,2,1,0:T(2,128)(2,1)} %bitcast.14) | data formatting | bytes 16777216
  20.6 10.5 %all_gather.7 = bf16[24,16,512]{2,1,0:T(8,128)(2,1)} all-gather(bf16[6,16,512]{2,1,0:T(8,128)(2,1)S(1)} %reshape.37), channel_id=1, replica_groups=mesh['groups'=2,'tenant'=4,'tensor'=4] {'tenant'}, dimensions={0}, use_global_device_ids=true | all-gather | bytes 491520 | tf_op jit(solution)/shard_map/all_gather | solution.py:296
  31.1 2.9 %all-gather.2.cloned.1.call-done = bf16[24,16,2048]{2,1,0:T(8,128)(2,1)} async-done(((bf16[6,16,2048]{2,1,0:T(8,128)(2,1)}), bf16[24,16,2048]{2,1,0:T(8,128)(2,1)}) %all-gather.2.cloned.1.call-update) | async-done | bytes 1572880 | tf_op jit(solution)/shard_map/all_gather | solution.py:295
  34.1 94.3 %shard_map.102 = (bf16[768,512]{1,0:T(8,128)(2,1)}, bf16[768,2048]{1,0:T(8,128)(2,1)}, f32[96,2048]{1,0:T(8,128)}, f32[96,512]{1,0:T(8,128)}) custom-call(bf16[768,8192]{1,0:T(8,128)(2,1)} %tokens.1, bf16[8192,512]{1,0:T(8,128)(2,1)} %bitcast.13, bf16[768,512]{1,0:T(8,128)(2,1)} %bitcast.15, bf16[384,2048]{1,0:T(8,128)(2,1)} %bitcast.16, ...), custom_call_target="tpu_custom_call" | custom-call | tf_op jit(solution)/shard_map/pallas_call | solution.py:309
  128.4 0.0 copy-start
  128.4 3.0 %reshape.39 = bf16[768,2,256]{2,1,0:T(2,128)(2,1)} reshape(bf16[768,512]{1,0:T(8,128)(2,1)} %get-tuple-element.8) | data formatting | bytes 1572864 | tf_op jit(solution)/shard_map/reshape | solution.py:353
  131.4 1.7 %reshape.41 = f32[6,16,2,256]{3,2,1,0:T(2,128)} reshape(f32[96,512]{1,0:T(8,128)} %get-tuple-element.11) | data formatting | bytes 393216 | tf_op jit(solution)/shard_map/reshape | solution.py:356
  133.1 4.0 %copy.18 = bf16[768,2048]{1,0:T(8,128)(2,1)} copy(bf16[768,2048]{1,0:T(8,128)(2,1)} %get-tuple-element.17) | data formatting | bytes 6291456
  137.1 0.0 copy-done
  137.1 0.9 copy.19
Async XLA Ops:
  7.2 26.9 %all-gather.2.cloned.1.call-start = ((), (), s32[]{:S(2)}) async-start(), calls=%async_computation | async-start | bytes 1966080 | tf_op jit(solution)/shard_map/all_gather | solution.py:295
  128.4 8.7 %copy-start = (f32[96,2048]{1,0:T(8,128)S(1)}, f32[96,2048]{1,0:T(8,128)}, u32[]{:S(2)}) copy-start(f32[96,2048]{1,0:T(8,128)} %get-tuple-element.10) | copy-start | bytes 2359300
Sparse Core Ops, SparseCore 0:
  9.6 24.4 all-gather.1

commit v3 on v2

--- a/solution.py
+++ b/solution.py
@@ -16,18 +16,20 @@
 
 
 def kernel(
-    sizes, tokens, weight, g_ref, a_ref, b_ref, want_ref,
+    sizes, tokens, weight, g_ref, a_own, b_own, want_ref,
     kv_ref, in_ref, ag_ref, bg_ref,
-    x_buf, wk_buf, acc, x_cols, w_buf, g_buf, total, rank_out, rank_in, grad_out, grad_in, back_ref,
+    x_buf, wk_buf, acc, x_cols, w_buf, g_buf, total, rank_out, rank_in, grad_out, grad_in, back_ref, a_ref, b_ref,
     x_sem, wk_sem, own_sem, w_send, w_recv, plane_send, sib_send,
     up_send, up_recv, down_send, down_recv, rank_send, rank_recv, grad_send, grad_recv,
+    a_send, a_recv, b_send, b_recv,
 ):
-    n, ng, nt, piece, rank, step = sizes
+    n, ng, nt, piece, rank, step, parts = sizes
     rows, width = tokens.shape
     wide = weight.shape[1]
     narrow = x_cols.shape[1]
     stored = a_ref.shape[0]
     owned = stored // nt
+    part_rows = rows // parts
     me = lax.axis_index("tensor")
     grp = lax.axis_index("groups")
     ten = lax.axis_index("tenant")
@@ -69,6 +71,12 @@
     for copy in load(0, 0):
         copy.start()
     own_w.start()
+
+    def held(ref, t):
+        return ref.at[pl.ds(pl.multiple_of(t * owned, owned), owned), :]
+
+    held(a_ref, ten)[...] = a_own[...]
+    held(b_ref, ten)[...] = b_own[...]
     pl.semaphore_wait(barrier, n - 1 + ng * nt - 1)
 
     def spot(z, p):
@@ -78,6 +86,22 @@
         return pltpu.make_async_remote_copy(
             src_ref=src, dst_ref=dst, send_sem=send, recv_sem=recv, device_id=device, device_id_type=MESH
         )
+
+    adapter_sends = []
+
+    def send_adapters(t, to, i):
+        for ref, send, recv in ((a_ref, a_send, a_recv), (b_ref, b_send, b_recv)):
+            copy = remote(held(ref, t), held(ref, t), send.at[i], recv.at[t], (grp, to, me))
+            copy.start()
+            adapter_sends.append(copy)
+
+    def wait_adapters(t):
+        for ref, send, recv in ((a_ref, a_send, a_recv), (b_ref, b_send, b_recv)):
+            remote(held(ref, t), held(ref, t), send.at[0], recv.at[t], (grp, side, me)).wait_recv()
+
+    send_adapters(ten, side, 0)
+    for dt in range(2, nt, 2):
+        send_adapters(ten, lax.rem(ten + dt, nt), dt)
 
     w_sends = []
     for k in range(1, n):
@@ -89,38 +113,70 @@
         copy.start()
         w_sends.append(copy)
 
-    def up(s):
-        o = jnp.maximum(me - s, 0)
-        src = g_ref if s == 0 else g_buf.at[o]
-        return (
-            jnp.logical_and(me >= s, me < n - 1),
-            remote(src, g_buf.at[o], up_send.at[s], up_recv.at[s], at_tensor(jnp.minimum(me + 1, n - 1))),
-        )
-
-    def down(s):
-        o = jnp.minimum(me + s, n - 1)
-        src = g_ref if s == 0 else g_buf.at[o]
-        return (
-            jnp.logical_and(me + s < n, me > 0),
-            remote(src, g_buf.at[o], down_send.at[s], down_recv.at[s], at_tensor(jnp.maximum(me - 1, 0))),
-        )
-
-    def push(s):
-        for ok, copy in (up(s), down(s)):
+    def cut(ref, c):
+        return ref.at[pl.ds(c * part_rows, part_rows), :]
+
+    def hop(s, c, origin, to, send, recv):
+        src = cut(g_ref, c) if s == 0 else cut(g_buf.at[origin], c)
+        i = s * parts + c
+        return remote(src, cut(g_buf.at[origin], c), send.at[i], recv.at[i], at_tensor(to))
+
+    def up(s, c):
+        copy = hop(s, c, jnp.maximum(me - s, 0), jnp.minimum(me + 1, n - 1), up_send, up_recv)
+        return jnp.logical_and(me >= s, me < n - 1), copy
+
+    def down(s, c):
+        copy = hop(s, c, jnp.minimum(me + s, n - 1), jnp.maximum(me - 1, 0), down_send, down_recv)
+        return jnp.logical_and(me + s < n, me > 0), copy
+
+    def push(s, c):
+        for ok, copy in (up(s, c), down(s, c)):
             pl.when(ok)(copy.start)
 
-    def arrived(s):
+    def arrived(s, c):
         low, high = me - 1 - s, me + 1 + s
         pl.when(low >= 0)(
-            remote(g_ref, g_buf.at[jnp.maximum(low, 0)], up_send.at[s], up_recv.at[s], at_tensor(jnp.maximum(me - 1, 0))).wait_recv
+            hop(s, c, jnp.maximum(low, 0), jnp.maximum(me - 1, 0), up_send, up_recv).wait_recv
         )
         pl.when(high < n)(
-            remote(g_ref, g_buf.at[jnp.minimum(high, n - 1)], down_send.at[s], down_recv.at[s], at_tensor(jnp.minimum(me + 1, n - 1))).wait_recv
+            hop(s, c, jnp.minimum(high, n - 1), jnp.minimum(me + 1, n - 1), down_send, down_recv).wait_recv
         )
 
-    push(0)
-
-    ids = lax.broadcasted_iota(jnp.int32, (stored, rows), 0) // rank
+    def relay(s):
+        for c in range(parts):
+            arrived(s, c)
+            push(s + 1, c)
+
+    for c in range(parts):
+        push(0, c)
+
+    chunks = width // step
+    acc[...] = jnp.zeros_like(acc)
+
+    def chunk(c, carry):
+        slot = lax.rem(c, 2)
+
+        @pl.when(c + 1 < chunks)
+        def _():
+            for copy in load(c + 1, 1 - slot):
+                copy.start()
+
+        for copy in load(c, slot):
+            copy.wait()
+        acc[...] += mm(x_buf[slot], wk_buf[slot], 1, 0)
+        return carry
+
+    half = chunks // 2
+    lax.fori_loop(0, half, chunk, 0)
+    for dt in range(2, nt, 2):
+        t2 = lax.rem(ten + dt, nt)
+        wait_adapters(t2)
+        send_adapters(t2, side, dt + 1)
+    lax.fori_loop(half, chunks, chunk, 0)
+    for dt in range(0, nt, 2):
+        wait_adapters(lax.rem(side + dt, nt))
+
+    ids = lax.broadcasted_iota(jnp.int32, (stored, 1), 0) // rank
     mask = ids == want_ref[...]
     fold = (
         lax.rem(lax.broadcasted_iota(jnp.int32, (stored, rank), 0), rank)
@@ -137,23 +193,22 @@
         copy.start()
         rank_sends.append(copy)
 
-    chunks = width // step
-    acc[...] = jnp.zeros_like(acc)
-
-    def chunk(c, carry):
-        slot = lax.rem(c, 2)
-
-        @pl.when(c + 1 < chunks)
-        def _():
-            for copy in load(c + 1, 1 - slot):
-                copy.start()
-
-        for copy in load(c, slot):
-            copy.wait()
-        acc[...] += mm(x_buf[slot], wk_buf[slot], 1, 0)
-        return carry
-
-    lax.fori_loop(0, chunks, chunk, 0)
+    tile = min(narrow, 512)
+
+    def add_block(o, g_block, first):
+        def body(c, carry):
+            cols = pl.ds(pl.multiple_of(c * tile, tile), tile)
+            term = mm(g_block[...], w_buf[o, cols, :], 1, 1)
+            if first:
+                total[:, cols] = term
+            else:
+                total[:, cols] += term
+            return carry
+
+        lax.fori_loop(0, narrow // tile, body, 0)
+
+    own_w.wait()
+    add_block(me, g_ref, True)
 
     plane_sends, sib_sends = [], []
 
@@ -166,7 +221,8 @@
         remote(spot(z, p), spot(z, p), sib_send.at[0], w_recv.at[z, p], (grp, side, me)).wait_recv()
 
     others = [(dg, dt) for dg in range(ng) for dt in range(0, nt, 2) if dg or dt]
-    for k in range(1, n):
+    near = sorted(range(1, n), key=lambda k: (min(k, n - k), k))
+    for k in near:
         z = line(k)
         wait_piece(z, plane)
         for dg, dt in others:
@@ -189,9 +245,10 @@
     shrink = jnp.where(mask, mm(fold, twice[:rank, :], 1, 0), 0.0).astype(BF16)
     back_ref[...] = jnp.where(mask, mm(fold, twice[rank:, :], 1, 0), 0.0).astype(BF16)
 
+    if n > 2:
+        relay(0)
     for p in range(nt):
-        part_rows = pl.ds(p * owned, owned)
-        grad_out[p, :, :narrow] = mm(back_ref[part_rows, :], x_cols[...], 1, 0).astype(BF16)
+        grad_out[p, :, :narrow] = mm(back_ref[pl.ds(p * owned, owned), :], x_cols[...], 1, 0).astype(BF16)
     spread = mm(shrink, g_ref[...], 1, 0).astype(BF16)
     for p in range(nt):
         grad_out[p, :, narrow:] = spread[p * owned : (p + 1) * owned, :]
@@ -203,26 +260,13 @@
         grad_sends.append(copy)
     kv_ref[...] = (acc[...] + mm(shrink, b_ref[...], 0, 0)).astype(BF16)
 
-    tile = min(narrow, 512)
-
-    def add_block(o, g_block, first):
-        def body(c, carry):
-            cols = pl.ds(pl.multiple_of(c * tile, tile), tile)
-            term = mm(g_block[...], w_buf[o, cols, :], 1, 1)
-            if first:
-                total[:, cols] = term + mm(back_ref[...], a_ref[:, cols], 0, 0)
-            else:
-                total[:, cols] += term
-            return carry
-
-        lax.fori_loop(0, narrow // tile, body, 0)
-
-    own_w.wait()
-    arrived(0)
-    if n > 2:
-        push(1)
-    add_block(me, g_ref, True)
-    for k in range(1, n):
+    def add_adapter(c, carry):
+        cols = pl.ds(pl.multiple_of(c * tile, tile), tile)
+        total[:, cols] += mm(back_ref[...], a_ref[:, cols], 0, 0)
+        return carry
+
+    lax.fori_loop(0, narrow // tile, add_adapter, 0)
+    for k in near:
         z = line(k)
         for dg, dt in others:
             g2, t2 = mate(dg, dt)
@@ -230,8 +274,7 @@
             wait_piece(z, p)
             to_side(z, p, len(sib_sends))
     for s in range(1, n - 2):
-        arrived(s)
-        push(s + 1)
+        relay(s)
     for k in range(1, n):
         z = line(k)
         for dg in range(ng):
@@ -268,15 +311,32 @@
     ag_ref[...] = ag
     bg_ref[...] = bg
 
-    arrived(n - 2)
-    use(n - 2)
-    in_ref[...] = total[...].astype(BF16)
-
-    for copy in w_sends + plane_sends + sib_sends + rank_sends + grad_sends:
+    def finish(o):
+        for c in range(parts):
+            arrived(n - 2, c)
+            span = pl.ds(c * part_rows, part_rows)
+
+            def body(i, carry):
+                cols = pl.ds(pl.multiple_of(i * tile, tile), tile)
+                term = mm(g_buf[o, span, :], w_buf[o, cols, :], 1, 1)
+                in_ref[span, cols] = (total[span, cols] + term).astype(BF16)
+                return carry
+
+            lax.fori_loop(0, narrow // tile, body, 0)
+
+    pl.when(me == n - 1)(lambda: finish(0))
+    pl.when(me == 0)(lambda: finish(n - 1))
+
+    @pl.when(jnp.logical_and(me > 0, me < n - 1))
+    def _():
+        in_ref[...] = total[...].astype(BF16)
+
+    for copy in w_sends + plane_sends + sib_sends + rank_sends + grad_sends + adapter_sends:
         copy.wait_send()
     for s in range(n - 1):
-        for ok, copy in (up(s), down(s)):
-            pl.when(ok)(copy.wait_send)
+        for c in range(parts):
+            for ok, copy in (up(s, c), down(s, c)):
+                pl.when(ok)(copy.wait_send)
 
 
 def local(tokens, kv_weight, cotangent, a_store, b_store, tile_tenant, tenant_place):
@@ -292,9 +352,7 @@
     ng = lax.axis_size("groups")
     piece = narrow // (ng * nt)
 
-    a_all = lax.all_gather(a_store, "tenant", axis=0, tiled=True).reshape(-1, narrow)
-    b_all = lax.all_gather(b_store.reshape(slots, rank, wide), "tenant", axis=0, tiled=True).reshape(-1, wide)
-    stored = a_all.shape[0]
+    stored = nt * slots * rank
     w_flat = kv_weight.reshape(model_width, wide)
     g_flat = cotangent.reshape(rows, wide)
     lookup = tile_tenant[:, None] == jnp.arange(tenants, dtype=jnp.int32)[None, :]
@@ -306,8 +364,9 @@
     hbm = pl.BlockSpec(memory_space=pl.ANY)
     dma = pltpu.SemaphoreType.DMA
     mates = ng * nt // 2
+    parts = 2
     kv, inp, ag, bg = pl.pallas_call(
-        functools.partial(kernel, (n, ng, nt, piece, rank, step)),
+        functools.partial(kernel, (n, ng, nt, piece, rank, step, parts)),
         out_shape=(
             jax.ShapeDtypeStruct((rows, wide), BF16),
             jax.ShapeDtypeStruct((rows, narrow), BF16),
@@ -329,6 +388,8 @@
             pltpu.VMEM((nt, slots * rank, narrow + wide), BF16),
             pltpu.VMEM((nt, slots * rank, narrow + wide), BF16),
             pltpu.VMEM((stored, rows), BF16),
+            pltpu.VMEM((stored, narrow), BF16),
+            pltpu.VMEM((stored, wide), BF16),
             dma((2,)),
             dma((2,)),
             dma((2,)),
@@ -336,19 +397,30 @@
             dma((n, ng * nt)),
             dma(((n - 1) * max(mates - 1, 1),)),
             dma(((n - 1) * mates,)),
+            dma((n * parts,)),
+            dma((n * parts,)),
+            dma((n * parts,)),
+            dma((n * parts,)),
             dma((n,)),
             dma((n,)),
-            dma((n,)),
-            dma((n,)),
-            dma((n,)),
-            dma((n,)),
+            dma((nt,)),
+            dma((nt,)),
+            dma((nt,)),
+            dma((nt,)),
             dma((nt,)),
             dma((nt,)),
         ],
         compiler_params=pltpu.CompilerParams(
             collective_id=0, has_side_effects=True, vmem_limit_bytes=60 * 1024 * 1024
         ),
-    )(tokens, w_flat, g_flat, a_all, b_all, want_rows)
+    )(
+        tokens,
+        w_flat,
+        g_flat,
+        a_store.reshape(slots * rank, narrow),
+        b_store.reshape(slots * rank, wide),
+        want_rows,
+    )
     return (
         kv.reshape(rows, 2, part_cols),
         inp,

time: 145 us -> 117 us (0.81)
  between operations: 14 us -> 0.65 us
  blocking collectives: 10.5 us -> 0 us
  waiting for transfers between devices: 3.59 us -> 0 us
    all_gather x1 -> x0, blocking collectives: 10.5 us -> none  [local(): lax.all_gather(b_store.reshape(slots, rank, wide), 'tenant', axis=0, tile...]
    all_gather x1 -> x0, waiting for transfers between devices: 2.91 us -> none  [local(): lax.all_gather(a_store, 'tenant', axis=0, tiled=True).reshape(-1, narrow)]
    unnamed x8 -> x9, local copies, waits for them, and re-layouts: 15.8 us -> 17.2 us
  transfers between devices with their start and end apart: 1 -> 0, of which waited for: 1 -> 0; matrix products, arithmetic and copies ran while one was open for 9% -> 0% of each run, Pallas kernels for 0% -> 0%
where the time goes in v3:
time: 117 us; the launch traced here: 116 us
  Pallas kernels  92.9 us (79%)
  local copies, waits for them, and re-layouts  22 us (19%)
    pallas_call x1, Pallas kernels, local(): pl.pallas_call(functools.partial(kernel, (n, ng, nt, piece, rank, step, p...  92.9 us
    unnamed x9, local copies, waits for them, and re-layouts  17.2 us
    reshape x1, local copies, waits for them, and re-layouts, local(): kv.reshape(rows, 2, part_cols)  2.99 us

profile of v3, /device:TPU:0, one launch (start us, length us, event | category | flops | bytes accessed | tf_op | source)
XLA Modules:
  0.0 116.3 jit_solution(15291703293722201521)
XLA Ops:
  0.6 0.9 select_reduce_fusion
  1.5 0.1 broadcast_bitcast_fusion
  1.6 0.6 copy.16
  2.1 1.5 %copy.13 = bf16[12,8,2,256]{3,1,2,0:T(8,128)(2,1)} copy(bf16[12,8,2,256]{3,2,1,0:T(2,128)(2,1)} %bitcast.22) | data formatting | bytes 196608
  3.7 2.2 %copy.12 = bf16[96,8,2,256]{3,1,2,0:T(8,128)(2,1)} copy(bf16[96,8,2,256]{3,2,1,0:T(2,128)(2,1)} %bitcast.18) | data formatting | bytes 1572864
  5.9 8.0 %copy.11 = bf16[1024,8,2,256]{3,1,2,0:T(8,128)(2,1)} copy(bf16[1024,8,2,256]{3,2,1,0:T(2,128)(2,1)} %bitcast.16) | data formatting | bytes 16777216
  13.9 92.9 %shard_map.102 = (bf16[768,512]{1,0:T(8,128)(2,1)}, bf16[768,2048]{1,0:T(8,128)(2,1)}, f32[96,2048]{1,0:T(8,128)}, f32[96,512]{1,0:T(8,128)}) custom-call(bf16[768,8192]{1,0:T(8,128)(2,1)} %tokens.1, bf16[8192,512]{1,0:T(8,128)(2,1)} %bitcast.15, bf16[768,512]{1,0:T(8,128)(2,1)} %bitcast.17, bf16[96,2048]{1,0:T(8,128)(2,1)} %bitcast.21, ...), custom_call_target="tpu_custom_call" | custom-call | tf_op jit(solution)/shard_map/pallas_call | solution.py:368
  106.8 0.0 copy-start
  106.8 3.0 %reshape.35 = bf16[768,2,256]{2,1,0:T(2,128)(2,1)} reshape(bf16[768,512]{1,0:T(8,128)(2,1)} %get-tuple-element.8) | data formatting | bytes 1572864 | tf_op jit(solution)/shard_map/reshape | solution.py:425
  109.8 1.7 %reshape.37 = f32[6,16,2,256]{3,2,1,0:T(2,128)} reshape(f32[96,512]{1,0:T(8,128)} %get-tuple-element.11) | data formatting | bytes 393216 | tf_op jit(solution)/shard_map/reshape | solution.py:428
  111.5 4.0 %copy.19 = bf16[768,2048]{1,0:T(8,128)(2,1)} copy(bf16[768,2048]{1,0:T(8,128)(2,1)} %get-tuple-element.17) | data formatting | bytes 6291456
  115.5 0.0 copy-done
  115.5 0.9 copy.20
Async XLA Ops:
  106.8 8.7 %copy-start = (f32[96,2048]{1,0:T(8,128)S(1)}, f32[96,2048]{1,0:T(8,128)}, u32[]{:S(2)}) copy-start(f32[96,2048]{1,0:T(8,128)} %get-tuple-element.10) | copy-start | bytes 2359300

commit v4 on v3

--- a/solution.py
+++ b/solution.py
@@ -18,10 +18,10 @@
 def kernel(
     sizes, tokens, weight, g_ref, a_own, b_own, want_ref,
     kv_ref, in_ref, ag_ref, bg_ref,
-    x_buf, wk_buf, acc, x_cols, w_buf, g_buf, total, rank_out, rank_in, grad_out, grad_in, back_ref, a_ref, b_ref,
+    x_buf, wk_buf, acc, x_cols, w_buf, g_buf, total, rank_out, rank_in, grad_out, grad_side, grad_in, back_ref, a_ref, b_ref,
     x_sem, wk_sem, own_sem, w_send, w_recv, plane_send, sib_send,
     up_send, up_recv, down_send, down_recv, rank_send, rank_recv, grad_send, grad_recv,
-    a_send, a_recv, b_send, b_recv,
+    a_send, a_recv, b_send, b_recv, side_recv,
 ):
     n, ng, nt, piece, rank, step, parts = sizes
     rows, width = tokens.shape
@@ -147,8 +147,54 @@
             arrived(s, c)
             push(s + 1, c)
 
-    for c in range(parts):
-        push(0, c)
+    others = [(dg, dt) for dg in range(ng) for dt in range(0, nt, 2) if dg or dt]
+
+    def to_side(z, p, i):
+        return remote(spot(z, p), spot(z, p), sib_send.at[i], w_recv.at[z, p], (grp, side, me))
+
+    def wait_piece(z, p):
+        to_side(z, p, 0).wait_recv()
+
+    def fan_out(z):
+        turn = lax.rem(z - me + n, n) - 1
+        copies = [to_side(z, plane, turn * (len(others) + 1))]
+        for i, (dg, dt) in enumerate(others):
+            g2, t2 = mate(dg, dt)
+            copies.append(
+                remote(
+                    spot(z, plane), spot(z, plane), plane_send.at[turn * len(others) + i], w_recv.at[z, plane], (g2, t2, me)
+                )
+            )
+        return copies
+
+    def pass_on(z):
+        turn = lax.rem(z - me + n, n) - 1
+        found = []
+        for i, (dg, dt) in enumerate(others):
+            g2, t2 = mate(dg, dt)
+            p = g2 * nt + t2
+            found.append((p, to_side(z, p, turn * (len(others) + 1) + 1 + i)))
+        return found
+
+    def both(distance, act):
+        low, high = me - distance, me + distance
+        pl.when(low >= 0)(lambda: act(jnp.maximum(low, 0)))
+        pl.when(high < n)(lambda: act(jnp.minimum(high, n - 1)))
+
+    def fan(z):
+        wait_piece(z, plane)
+        for copy in fan_out(z)[::-1]:
+            copy.start()
+
+    def hand(z):
+        for p, copy in pass_on(z):
+            wait_piece(z, p)
+            copy.start()
+
+    def settle(z):
+        for dg in range(ng):
+            for dt in range(0, nt, 2):
+                wait_piece(z, lax.rem(grp + dg, ng) * nt + lax.rem(side + dt, nt))
 
     chunks = width // step
     acc[...] = jnp.zeros_like(acc)
@@ -172,7 +218,12 @@
         t2 = lax.rem(ten + dt, nt)
         wait_adapters(t2)
         send_adapters(t2, side, dt + 1)
+    for c in range(parts):
+        push(0, c)
+    both(1, fan)
     lax.fori_loop(half, chunks, chunk, 0)
+    if n > 2:
+        both(2, fan)
     for dt in range(0, nt, 2):
         wait_adapters(lax.rem(side + dt, nt))
 
@@ -207,32 +258,11 @@
 
         lax.fori_loop(0, narrow // tile, body, 0)
 
+    for d in range(3, n):
+        both(d, fan)
     own_w.wait()
     add_block(me, g_ref, True)
-
-    plane_sends, sib_sends = [], []
-
-    def to_side(z, p, i):
-        copy = remote(spot(z, p), spot(z, p), sib_send.at[i], w_recv.at[z, p], (grp, side, me))
-        copy.start()
-        sib_sends.append(copy)
-
-    def wait_piece(z, p):
-        remote(spot(z, p), spot(z, p), sib_send.at[0], w_recv.at[z, p], (grp, side, me)).wait_recv()
-
-    others = [(dg, dt) for dg in range(ng) for dt in range(0, nt, 2) if dg or dt]
-    near = sorted(range(1, n), key=lambda k: (min(k, n - k), k))
-    for k in near:
-        z = line(k)
-        wait_piece(z, plane)
-        for dg, dt in others:
-            g2, t2 = mate(dg, dt)
-            copy = remote(
-                spot(z, plane), spot(z, plane), plane_send.at[len(plane_sends)], w_recv.at[z, plane], (g2, t2, me)
-            )
-            copy.start()
-            plane_sends.append(copy)
-        to_side(z, plane, len(sib_sends))
+    both(1, hand)
 
     rank_in[me] = rank_out[...]
     for k in range(1, n):
@@ -245,20 +275,29 @@
     shrink = jnp.where(mask, mm(fold, twice[:rank, :], 1, 0), 0.0).astype(BF16)
     back_ref[...] = jnp.where(mask, mm(fold, twice[rank:, :], 1, 0), 0.0).astype(BF16)
 
-    if n > 2:
-        relay(0)
     for p in range(nt):
         grad_out[p, :, :narrow] = mm(back_ref[pl.ds(p * owned, owned), :], x_cols[...], 1, 0).astype(BF16)
     spread = mm(shrink, g_ref[...], 1, 0).astype(BF16)
     for p in range(nt):
         grad_out[p, :, narrow:] = spread[p * owned : (p + 1) * owned, :]
     grad_sends = []
-    for dt in range(1, nt):
-        t2 = lax.rem(ten + dt, nt)
-        copy = remote(grad_out.at[t2], grad_in.at[ten], grad_send.at[dt], grad_recv.at[ten], (grp, t2, me))
+    for dt in range(0, nt, 2):
+        t2 = lax.rem(side + dt, nt)
+        copy = remote(grad_out.at[t2], grad_side.at[t2], grad_send.at[dt], side_recv.at[t2], (grp, side, me))
         copy.start()
         grad_sends.append(copy)
     kv_ref[...] = (acc[...] + mm(shrink, b_ref[...], 0, 0)).astype(BF16)
+
+    if n > 2:
+        relay(0)
+    for dt in range(0, nt, 2):
+        t2 = lax.rem(ten + dt, nt)
+        remote(grad_out.at[t2], grad_side.at[t2], grad_send.at[0], side_recv.at[t2], (grp, side, me)).wait_recv()
+        if dt:
+            grad_out[t2] = (grad_out[t2].astype(F32) + grad_side[t2].astype(F32)).astype(BF16)
+            copy = remote(grad_out.at[t2], grad_in.at[ten], grad_send.at[dt + 1], grad_recv.at[ten], (grp, t2, me))
+            copy.start()
+            grad_sends.append(copy)
 
     def add_adapter(c, carry):
         cols = pl.ds(pl.multiple_of(c * tile, tile), tile)
@@ -266,23 +305,6 @@
         return carry
 
     lax.fori_loop(0, narrow // tile, add_adapter, 0)
-    for k in near:
-        z = line(k)
-        for dg, dt in others:
-            g2, t2 = mate(dg, dt)
-            p = g2 * nt + t2
-            wait_piece(z, p)
-            to_side(z, p, len(sib_sends))
-    for s in range(1, n - 2):
-        relay(s)
-    for k in range(1, n):
-        z = line(k)
-        for dg in range(ng):
-            for dt in range(0, nt, 2):
-                g2 = lax.rem(grp + dg, ng)
-                t2 = lax.rem(side + dt, nt)
-                wait_piece(z, g2 * nt + t2)
-
     def use(s):
         low, high = me - 1 - s, me + 1 + s
 
@@ -296,20 +318,25 @@
             o = jnp.minimum(high, n - 1)
             add_block(o, g_buf.at[o], False)
 
+    for d in range(2, n):
+        both(d, hand)
     for s in range(n - 2):
+        if s:
+            relay(s)
+        both(s + 1, settle)
         use(s)
 
-    grad_in[ten] = grad_out[ten]
-    for dt in range(1, nt):
+    ag = grad_out[ten, :, :narrow].astype(F32) + grad_side[ten, :, :narrow].astype(F32)
+    bg = grad_out[ten, :, narrow:].astype(F32) + grad_side[ten, :, narrow:].astype(F32)
+    for dt in range(2, nt, 2):
         t2 = lax.rem(ten + dt, nt)
-        remote(grad_out.at[t2], grad_in.at[t2], grad_send.at[dt], grad_recv.at[t2], (grp, t2, me)).wait_recv()
-    ag = grad_in[0, :, :narrow].astype(F32)
-    bg = grad_in[0, :, narrow:].astype(F32)
-    for p in range(1, nt):
-        ag = ag + grad_in[p, :, :narrow].astype(F32)
-        bg = bg + grad_in[p, :, narrow:].astype(F32)
+        remote(grad_out.at[t2], grad_in.at[t2], grad_send.at[0], grad_recv.at[t2], (grp, t2, me)).wait_recv()
+        ag = ag + grad_in[t2, :, :narrow].astype(F32)
+        bg = bg + grad_in[t2, :, narrow:].astype(F32)
     ag_ref[...] = ag
     bg_ref[...] = bg
+
+    both(n - 1, settle)
 
     def finish(o):
         for c in range(parts):
@@ -331,7 +358,11 @@
     def _():
         in_ref[...] = total[...].astype(BF16)
 
-    for copy in w_sends + plane_sends + sib_sends + rank_sends + grad_sends + adapter_sends:
+    for k in range(1, n):
+        z = line(k)
+        for copy in fan_out(z) + [copy for _, copy in pass_on(z)]:
+            copy.wait_send()
+    for copy in w_sends + rank_sends + grad_sends + adapter_sends:
         copy.wait_send()
     for s in range(n - 1):
         for c in range(parts):
@@ -387,6 +418,7 @@
             pltpu.VMEM((n, 2 * rank, rows), BF16),
             pltpu.VMEM((nt, slots * rank, narrow + wide), BF16),
             pltpu.VMEM((nt, slots * rank, narrow + wide), BF16),
+            pltpu.VMEM((nt, slots * rank, narrow + wide), BF16),
             pltpu.VMEM((stored, rows), BF16),
             pltpu.VMEM((stored, narrow), BF16),
             pltpu.VMEM((stored, wide), BF16),
@@ -403,6 +435,7 @@
             dma((n * parts,)),
             dma((n,)),
             dma((n,)),
+            dma((nt,)),
             dma((nt,)),
             dma((nt,)),
             dma((nt,)),

time: 117 us -> 120 us (1.026)
  Pallas kernels: 92.9 us -> 95.8 us
    pallas_call x1, Pallas kernels: 92.9 us -> 95.8 us  [local(): pl.pallas_call(functools.partial(kernel, (n, ng, nt, piece, rank, step, p...]
where the time goes in v4:
time: 120 us; the launch traced here: 119 us
  Pallas kernels  95.8 us (80%)
  local copies, waits for them, and re-layouts  22 us (18%)
    pallas_call x1, Pallas kernels, local(): pl.pallas_call(functools.partial(kernel, (n, ng, nt, piece, rank, step, p...  95.8 us
    unnamed x9, local copies, waits for them, and re-layouts  17.2 us
    reshape x1, local copies, waits for them, and re-layouts, local(): kv.reshape(rows, 2, part_cols)  2.99 us

profile of v4, /device:TPU:0, one launch (start us, length us, event | category | flops | bytes accessed | tf_op | source)
XLA Modules:
  0.0 119.2 jit_solution(11084724782431938241)
XLA Ops:
  0.6 0.9 select_reduce_fusion
  1.5 0.1 broadcast_bitcast_fusion
  1.6 0.6 copy.16
  2.1 1.5 %copy.13 = bf16[12,8,2,256]{3,1,2,0:T(8,128)(2,1)} copy(bf16[12,8,2,256]{3,2,1,0:T(2,128)(2,1)} %bitcast.22) | data formatting | bytes 196608
  3.7 2.2 %copy.12 = bf16[96,8,2,256]{3,1,2,0:T(8,128)(2,1)} copy(bf16[96,8,2,256]{3,2,1,0:T(2,128)(2,1)} %bitcast.18) | data formatting | bytes 1572864
  5.9 8.0 %copy.11 = bf16[1024,8,2,256]{3,1,2,0:T(8,128)(2,1)} copy(bf16[1024,8,2,256]{3,2,1,0:T(2,128)(2,1)} %bitcast.16) | data formatting | bytes 16777216
  13.9 95.8 %shard_map.102 = (bf16[768,512]{1,0:T(8,128)(2,1)}, bf16[768,2048]{1,0:T(8,128)(2,1)}, f32[96,2048]{1,0:T(8,128)}, f32[96,512]{1,0:T(8,128)}) custom-call(bf16[768,8192]{1,0:T(8,128)(2,1)} %tokens.1, bf16[8192,512]{1,0:T(8,128)(2,1)} %bitcast.15, bf16[768,512]{1,0:T(8,128)(2,1)} %bitcast.17, bf16[96,2048]{1,0:T(8,128)(2,1)} %bitcast.21, ...), custom_call_target="tpu_custom_call" | custom-call | tf_op jit(solution)/shard_map/pallas_call | solution.py:399
  109.7 0.0 copy-start
  109.7 3.0 %reshape.35 = bf16[768,2,256]{2,1,0:T(2,128)(2,1)} reshape(bf16[768,512]{1,0:T(8,128)(2,1)} %get-tuple-element.8) | data formatting | bytes 1572864 | tf_op jit(solution)/shard_map/reshape | solution.py:458
  112.7 1.7 %reshape.37 = f32[6,16,2,256]{3,2,1,0:T(2,128)} reshape(f32[96,512]{1,0:T(8,128)} %get-tuple-element.11) | data formatting | bytes 393216 | tf_op jit(solution)/shard_map/reshape | solution.py:461
  114.4 4.0 %copy.19 = bf16[768,2048]{1,0:T(8,128)(2,1)} copy(bf16[768,2048]{1,0:T(8,128)(2,1)} %get-tuple-element.17) | data formatting | bytes 6291456
  118.4 0.0 copy-done
  118.4 0.9 copy.20
Async XLA Ops:
  109.7 8.7 %copy-start = (f32[96,2048]{1,0:T(8,128)S(1)}, f32[96,2048]{1,0:T(8,128)}, u32[]{:S(2)}) copy-start(f32[96,2048]{1,0:T(8,128)} %get-tuple-element.10) | copy-start | bytes 2359300

commit v5 on v4

--- a/solution.py
+++ b/solution.py
@@ -147,6 +147,9 @@
             arrived(s, c)
             push(s + 1, c)
 
+    for c in range(parts):
+        push(0, c)
+
     others = [(dg, dt) for dg in range(ng) for dt in range(0, nt, 2) if dg or dt]
 
     def to_side(z, p, i):
@@ -218,8 +221,6 @@
         t2 = lax.rem(ten + dt, nt)
         wait_adapters(t2)
         send_adapters(t2, side, dt + 1)
-    for c in range(parts):
-        push(0, c)
     both(1, fan)
     lax.fori_loop(half, chunks, chunk, 0)
     if n > 2:
@@ -275,6 +276,8 @@
     shrink = jnp.where(mask, mm(fold, twice[:rank, :], 1, 0), 0.0).astype(BF16)
     back_ref[...] = jnp.where(mask, mm(fold, twice[rank:, :], 1, 0), 0.0).astype(BF16)
 
+    if n > 2:
+        relay(0)
     for p in range(nt):
         grad_out[p, :, :narrow] = mm(back_ref[pl.ds(p * owned, owned), :], x_cols[...], 1, 0).astype(BF16)
     spread = mm(shrink, g_ref[...], 1, 0).astype(BF16)
@@ -288,8 +291,6 @@
         grad_sends.append(copy)
     kv_ref[...] = (acc[...] + mm(shrink, b_ref[...], 0, 0)).astype(BF16)
 
-    if n > 2:
-        relay(0)
     for dt in range(0, nt, 2):
         t2 = lax.rem(ten + dt, nt)
         remote(grad_out.at[t2], grad_side.at[t2], grad_send.at[0], side_recv.at[t2], (grp, side, me)).wait_recv()

time: 120 us -> 117 us (0.975)
  Pallas kernels: 95.8 us -> 92.9 us
    pallas_call x1, Pallas kernels: 95.8 us -> 92.9 us  [local(): pl.pallas_call(functools.partial(kernel, (n, ng, nt, piece, rank, step, p...]
where the time goes in v5:
time: 117 us; the launch traced here: 116 us
  Pallas kernels  92.9 us (79%)
  local copies, waits for them, and re-layouts  22 us (19%)
    pallas_call x1, Pallas kernels, local(): pl.pallas_call(functools.partial(kernel, (n, ng, nt, piece, rank, step, p...  92.9 us
    unnamed x9, local copies, waits for them, and re-layouts  17.2 us
    reshape x1, local copies, waits for them, and re-layouts, local(): kv.reshape(rows, 2, part_cols)  2.99 us

profile of v5, /device:TPU:0, one launch (start us, length us, event | category | flops | bytes accessed | tf_op | source)
XLA Modules:
  0.0 116.4 jit_solution(1152711128682244623)
XLA Ops:
  0.6 0.9 select_reduce_fusion
  1.5 0.1 broadcast_bitcast_fusion
  1.6 0.6 copy.16
  2.1 1.5 %copy.13 = bf16[12,8,2,256]{3,1,2,0:T(8,128)(2,1)} copy(bf16[12,8,2,256]{3,2,1,0:T(2,128)(2,1)} %bitcast.22) | data formatting | bytes 196608
  3.7 2.2 %copy.12 = bf16[96,8,2,256]{3,1,2,0:T(8,128)(2,1)} copy(bf16[96,8,2,256]{3,2,1,0:T(2,128)(2,1)} %bitcast.18) | data formatting | bytes 1572864
  5.9 8.0 %copy.11 = bf16[1024,8,2,256]{3,1,2,0:T(8,128)(2,1)} copy(bf16[1024,8,2,256]{3,2,1,0:T(2,128)(2,1)} %bitcast.16) | data formatting | bytes 16777216
  13.9 92.9 %shard_map.102 = (bf16[768,512]{1,0:T(8,128)(2,1)}, bf16[768,2048]{1,0:T(8,128)(2,1)}, f32[96,2048]{1,0:T(8,128)}, f32[96,512]{1,0:T(8,128)}) custom-call(bf16[768,8192]{1,0:T(8,128)(2,1)} %tokens.1, bf16[8192,512]{1,0:T(8,128)(2,1)} %bitcast.15, bf16[768,512]{1,0:T(8,128)(2,1)} %bitcast.17, bf16[96,2048]{1,0:T(8,128)(2,1)} %bitcast.21, ...), custom_call_target="tpu_custom_call" | custom-call | tf_op jit(solution)/shard_map/pallas_call | solution.py:400
  106.8 0.0 copy-start
  106.8 3.0 %reshape.35 = bf16[768,2,256]{2,1,0:T(2,128)(2,1)} reshape(bf16[768,512]{1,0:T(8,128)(2,1)} %get-tuple-element.8) | data formatting | bytes 1572864 | tf_op jit(solution)/shard_map/reshape | solution.py:459
  109.8 1.7 %reshape.37 = f32[6,16,2,256]{3,2,1,0:T(2,128)} reshape(f32[96,512]{1,0:T(8,128)} %get-tuple-element.11) | data formatting | bytes 393216 | tf_op jit(solution)/shard_map/reshape | solution.py:462
  111.5 4.0 %copy.19 = bf16[768,2048]{1,0:T(8,128)(2,1)} copy(bf16[768,2048]{1,0:T(8,128)(2,1)} %get-tuple-element.17) | data formatting | bytes 6291456
  115.5 0.0 copy-done
  115.5 0.9 copy.20
Async XLA Ops:
  106.8 8.7 %copy-start = (f32[96,2048]{1,0:T(8,128)S(1)}, f32[96,2048]{1,0:T(8,128)}, u32[]{:S(2)}) copy-start(f32[96,2048]{1,0:T(8,128)} %get-tuple-element.10) | copy-start | bytes 2359300
